TPU v7x, 256 devices: a whole 4x4x8 slice. The times are simulated.
256 devices in a mesh: dap: 128 (over x_lo, y, z, core), dp: 2 (over x_hi).
Axes of the slice: x: 4 (x_hi: 2, x_lo: 2; x = x_hi * 2 + x_lo), y: 4, z: 8, core: 2. Of those that a mesh axis runs over, the one named last changes fastest.
Arguments:
- aligned_rows: bfloat16 [256, 512, 256], P(('dp', 'dap')), parts along dimension 0, may hold values from -6 to 6
- asking_projection: bfloat16 [256, 256], replicated, may hold values from -1.5 to 1.5
- lookup_projection: bfloat16 [256, 256], replicated, may hold values from -0.25 to 0.25
- content_projection: bfloat16 [256, 256], replicated, may hold values from -0.375 to 0.375
- sigmoid_projection: bfloat16 [256, 256], replicated, may hold values from -0.375 to 0.375
- sigmoid_shift: float32 [256], replicated, may hold values from -2 to 2
- result_projection: bfloat16 [256, 256], replicated, may hold values from -0.375 to 0.375
- tensor_mean_projections: bfloat16 [256, 64], replicated, may hold values from -0.375 to 0.375
- twofold_projection: bfloat16 [1024, 128], replicated, may hold values from -0.1875 to 0.1875
- refreshed_rows_adjoint: bfloat16 [256, 512, 256], P(('dp', 'dap')), parts along dimension 0, may hold values from -6 to 6
- twofold_change_adjoint: bfloat16 [1024, 512, 128], P(('dp', 'dap')), parts along dimension 0, may hold values from -96 to 96
Outputs:
- entering_rows_derivative: bfloat16 [256, 512, 256], P(('dp', 'dap')), parts along dimension 0
- pair_weight_grad: float32 [2048, 128], P('dp'), parts along dimension 0
- outer_weight_grad: float32 [512, 64], P('dp'), parts along dimension 0
- right_factor_grad: float32 [256, 512, 32], P('dp', 'dap'), parts along dimension 0
There are 2 independent parts, one for each index of `dp`. A program takes and returns all parts, laid end to end along the dimension named above; an argument that names none is the same for every part. Nothing has to cross between parts.
All inputs are finite; a program needn't handle non-finite values.
Results may differ from a plain program's by a relative error of at most 0.035.
Values may be sent and summed in bfloat16 or wider, within the bound.
A program may use at most 128 MiB of HBM per device.

v0:
```python
import jax
import jax.numpy as jnp
from jax import lax
from jax.sharding import PartitionSpec as P

NUM_ATTENDERS = 8
PER_HEAD_DIM = 32


def layer_standardize(values):
    wide = values.astype(jnp.float32)
    average = jnp.mean(wide, axis=-1, keepdims=True)
    centred = wide - average
    variance = jnp.mean(centred * centred, axis=-1, keepdims=True)
    return (centred * lax.rsqrt(variance + 1e-05)).astype(jnp.bfloat16)


def column_self_attention(
    alignment_block,
    asking_projection,
    lookup_projection,
    content_projection,
    sigmoid_projection,
    sigmoid_shift,
    result_projection,
):
    sequence_total, residue_total, channel_width = alignment_block.shape
    normalised_rows = layer_standardize(alignment_block).reshape(
        sequence_total * residue_total, channel_width
    )

    def project(weight):
        return jnp.dot(normalised_rows, weight, preferred_element_type=jnp.float32)

    head_shape = (sequence_total, residue_total, NUM_ATTENDERS, PER_HEAD_DIM)
    query_heads = (
        (project(asking_projection) * PER_HEAD_DIM ** (-0.5))
        .astype(jnp.bfloat16)
        .reshape(head_shape)
    )
    key_heads = project(lookup_projection).astype(jnp.bfloat16).reshape(head_shape)
    value_heads = project(content_projection).astype(jnp.bfloat16).reshape(head_shape)
    gating = jax.nn.sigmoid(project(sigmoid_projection) + sigmoid_shift)
    scores = jnp.einsum(
        "schd,tchd->chst", query_heads, key_heads, preferred_element_type=jnp.float32
    )
    weights = jax.nn.softmax(scores, axis=-1).astype(jnp.bfloat16)
    attended = jnp.einsum(
        "chst,tchd->schd", weights, value_heads, preferred_element_type=jnp.float32
    )
    gated = (
        attended.reshape(sequence_total * residue_total, NUM_ATTENDERS * PER_HEAD_DIM) * gating
    ).astype(jnp.bfloat16)
    return jnp.dot(gated, result_projection, preferred_element_type=jnp.float32).reshape(
        sequence_total, residue_total, channel_width
    )


def contract_rows(lhs, rhs):
    return lax.dot_general(lhs, rhs, (((0,), (0,)), ((), ())), preferred_element_type=jnp.float32)


def body(
    aligned_rows,
    asking_projection,
    lookup_projection,
    content_projection,
    sigmoid_projection,
    sigmoid_shift,
    result_projection,
    tensor_mean_projections,
    twofold_projection,
    refreshed_rows_adjoint,
    twofold_change_adjoint,
):
    columns, incoming = (
        lax.all_to_all(aligned_rows, "dap", split_axis=1, concat_axis=0, tiled=True),
        lax.all_to_all(refreshed_rows_adjoint, "dap", split_axis=1, concat_axis=0, tiled=True),
    )
    sequence_total, residue_total, channel_width = columns.shape
    factor_width = tensor_mean_projections.shape[1] // 2
    pair_chan = twofold_change_adjoint.shape[2]

    def apply_column_heads(alignment_block):
        return column_self_attention(
            alignment_block,
            asking_projection,
            lookup_projection,
            content_projection,
            sigmoid_projection,
            sigmoid_shift,
            result_projection,
        )

    attn_out, attention_pullback = jax.vjp(apply_column_heads, columns)
    updated_alignment = (columns.astype(jnp.float32) + attn_out).astype(jnp.bfloat16)
    normalised_rows, norm_vjp = jax.vjp(layer_standardize, updated_alignment)
    projected_halves = jnp.dot(
        normalised_rows.reshape(-1, channel_width),
        tensor_mean_projections,
        preferred_element_type=jnp.float32,
    )
    projected_halves = projected_halves.astype(jnp.bfloat16).reshape(
        sequence_total, residue_total, 2 * factor_width
    )
    left_factor = projected_halves[..., :factor_width]
    right_factor = projected_halves[..., factor_width:]
    right_whole = lax.all_gather(right_factor, "dap", axis=1, tiled=True)
    outer = (
        jnp.einsum("sic,sje->ijce", left_factor, right_whole, preferred_element_type=jnp.float32)
        / sequence_total
    ).astype(jnp.bfloat16)
    flat_rows = twofold_change_adjoint.reshape(-1, pair_chan)
    pair_grad = (
        jnp.dot(flat_rows, twofold_projection.T, preferred_element_type=jnp.float32)
        / sequence_total
    ).astype(jnp.bfloat16)
    pair_grad = pair_grad.reshape(
        residue_total, twofold_change_adjoint.shape[1], factor_width, factor_width
    )
    pair_update_gradient = contract_rows(outer.reshape(-1, factor_width * factor_width), flat_rows)
    first_half_derivative = jnp.einsum(
        "ijce,sje->sic", pair_grad, right_whole, preferred_element_type=jnp.float32
    ).astype(jnp.bfloat16)
    summed = lax.psum_scatter(
        jnp.einsum("sic,ijce->jse", left_factor, pair_grad, preferred_element_type=jnp.float32),
        "dap",
        scatter_dimension=0,
        tiled=True,
    )
    right_sums = summed.transpose(1, 0, 2)
    grad_right = right_sums.astype(jnp.bfloat16)
    halves_derivative = jnp.concatenate([first_half_derivative, grad_right], axis=-1).reshape(
        -1, 2 * factor_width
    )
    tensor_mean_derivative = contract_rows(
        normalised_rows.reshape(-1, channel_width), halves_derivative
    )
    normalised_derivative = jnp.dot(
        halves_derivative, tensor_mean_projections.T, preferred_element_type=jnp.float32
    )
    normalised_derivative = normalised_derivative.astype(jnp.bfloat16).reshape(
        sequence_total, residue_total, channel_width
    )
    (grad_updated,) = norm_vjp(normalised_derivative)
    grad_mid = (incoming.astype(jnp.float32) + grad_updated.astype(jnp.float32)).astype(
        jnp.bfloat16
    )
    (grad_attn,) = attention_pullback(grad_mid.astype(jnp.float32))
    column_gradients = (grad_mid.astype(jnp.float32) + grad_attn.astype(jnp.float32)).astype(
        jnp.bfloat16
    )
    pair_update_gradient, tensor_mean_derivative = lax.psum(
        (pair_update_gradient, tensor_mean_derivative), "dap"
    )
    entering_rows_derivative = lax.all_to_all(
        column_gradients, "dap", split_axis=0, concat_axis=1, tiled=True
    )
    return (entering_rows_derivative, pair_update_gradient, tensor_mean_derivative, right_sums)


def solution(mesh):
    in_specs = (
        P(("dp", "dap"), None, None),
        P(),
        P(),
        P(),
        P(),
        P(),
        P(),
        P(),
        P(),
        P(("dp", "dap"), None, None),
        P(("dp", "dap"), None, None),
    )
    out_specs = (P(("dp", "dap"), None, None), P("dp", None), P("dp", None), P("dp", "dap", None))
    return jax.shard_map(body, mesh=mesh, in_specs=in_specs, out_specs=out_specs, check_vma=False)
```

profile of v0, /device:TPU:1, one launch (start us, length us, event | category | flops | bytes accessed | tf_op | source)
XLA Modules:
  0.0 1919.8 jit_solution(3838548745665061324)
XLA Ops:
  7.2 1.4 copy.139
  9.2 2.2 reduce.9
  11.6 28.3 %all_to_all.30 = bf16[128,2,512]{2,1,0:T(2,128)(2,1)S(1)} all-to-all(bf16[128,2,512]{2,1,0:T(2,128)(2,1)S(1)} %reshape.256), channel_id=1, replica_groups=mesh['dap'=128,'dp'=2] {'dap'}, dimensions={0} | all-to-all | bytes 524288 | tf_op jit(solution)/shard_map/all_to_all | solution.py:77
  42.0 1.1 copy.82
  43.8 1.8 copy.83
  46.4 1.1 copy.84
  47.5 1.8 fusion.76
  49.6 1.0 copy-done.1
  50.6 1.2 convolution_bitcast_fusion.1
  51.8 3.9 copy.86
  55.7 2.1 reshape.232
  57.9 1.4 fusion.13
  60.1 1.0 convert_reduce_fusion
  62.6 1.0 convolution_convert_fusion.12
  63.6 1.0 copy.87
  65.4 1.6 copy.88
  67.4 4.2 multiply_convert_fusion.1
  71.7 6.5 copy.89
  78.1 7.9 reshape.235
  86.1 28.8 %copy.93 = bf16[4,512,32,32]{2,3,0,1:T(8,128)(2,1)} copy(bf16[4,512,32,32]{1,0,3,2:T(4,128)(2,1)} %reshape.235) | data formatting | bytes 8388608 | tf_op jit(solution)/shard_map/reshape | solution.py:118
  114.9 11.6 convolution_bitcast_fusion
  126.5 1.4 copy.140
  127.9 2.9 reduce.8
  130.8 1.8 reshape.254
  132.6 6.6 all-to-all-start
  139.3 17.5 copy.111
  156.9 1.0 reshape.245
  160.1 1.0 reshape.237
  161.1 2.3 reshape.255
  164.3 2.0 reshape.242
  166.9 112.1 %all-gather.2.cloned.1.call-done = bf16[128,512,32]{0,2,1:T(8,128)(2,1)} async-done(((bf16[128,4,32]{0,2,1:T(8,128)(2,1)}), bf16[128,512,32]{0,2,1:T(8,128)(2,1)}) %all-gather.2.cloned.1.call-update) | async-done | bytes 4194320 | tf_op jit(solution)/shard_map/all_gather | solution.py:108
  278.9 7.1 fusion.1
  286.0 3.2 copy.107
  289.3 1.4 copy.123
  290.7 2.1 fusion.78
  292.7 11.7 fusion.26
  304.4 547.0 %reduce-scatter.2.cloned.1.call-done = f32[4,128,32]{1,2,0:T(8,128)} async-done(((f32[512,128,32]{1,2,0:T(8,128)}), f32[4,128,32]{1,2,0:T(8,128)}) %reduce-scatter.2.cloned.1.call-update) | async-done | bytes 65552 | tf_op jit(solution)/shard_map/reduce_scatter | solution.py:125
  853.1 1.4 fusion.33
  855.7 1.3 fusion.68
  857.1 2.7 fusion.77
  859.7 2.6 reshape.238
  862.4 2.9 copy.95
  865.3 2.7 fusion.25
  868.0 1.6 fusion.9
  869.7 1.4 fusion.21
  871.0 1.2 fusion.16
  873.0 2.4 copy.102
  875.4 1.4 reshape.240
  876.8 2.4 copy.97
  879.2 1.4 reshape.239
  880.7 2.0 convolution_convert_fusion.5
  882.7 3.3 copy.105
  886.0 2.6 mul.188
  888.6 1.2 fusion.79
  889.9 1.3 fusion.20
  891.2 1.4 fusion.41
  894.3 1.6 multiply_multiply_fusion.1
  895.9 2.0 multiply_convert_fusion.2
  897.9 1.6 convolution_bitcast_fusion.2
  900.2 2.8 add_convert_fusion
  903.0 24.8 %all_to_all.31 = bf16[128,4,256]{2,1,0:T(4,128)(2,1)S(1)} all-to-all(bf16[128,4,256]{2,1,0:T(4,128)(2,1)S(1)} %add_convert_fusion), channel_id=1, replica_groups=mesh['dap'=128,'dp'=2] {'dap'}, dimensions={0} | all-to-all | bytes 524288 | tf_op jit(solution)/shard_map/all_to_all | solution.py:156
  928.5 981.1 %all-reduce.3.cloned.1.call-done = (f32[1024,128]{1,0:T(8,128)}, f32[256,64]{0,1:T(8,128)}) async-done(((f32[1024,128]{1,0:T(8,128)}, f32[256,64]{0,1:T(8,128)}), (f32[1024,128]{1,0:T(8,128)}, f32[256,64]{0,1:T(8,128)})) %all-reduce.3.cloned.1.call-update) | async-done | bytes 589840 | tf_op jit(solution)/shard_map/psum | solution.py:153
  1909.7 1.9 copy.143
  1911.5 1.5 copy.144
  (129 shorter events, 18.8 us)
Async XLA Ops:
  7.2 60.3 %copy-start = (bf16[4,512,128]{2,1,0:T(8,128)(2,1)S(1)}, bf16[4,512,128]{2,1,0:T(8,128)(2,1)}, u32[]{:S(2)}) copy-start(bf16[4,512,128]{2,1,0:T(8,128)(2,1)} %param.21) | copy-start | bytes 1572868
  7.2 34.0 %copy-start.20 = (bf16[256,256]{1,0:T(8,128)(2,1)S(1)}, bf16[256,256]{1,0:T(8,128)(2,1)}, u32[]{:S(2)}) copy-start(bf16[256,256]{1,0:T(8,128)(2,1)} %param.12) | copy-start | bytes 393220
  7.2 35.9 %copy-start.22 = (bf16[256,256]{1,0:T(8,128)(2,1)S(1)}, bf16[256,256]{1,0:T(8,128)(2,1)}, u32[]{:S(2)}) copy-start(bf16[256,256]{1,0:T(8,128)(2,1)} %param.13) | copy-start | bytes 393220
  7.2 271.7 %all-gather.2.cloned.1.call-start = ((), (), s32[]{:S(2)}) async-start(), calls=%async_computation.4 | async-start | bytes 4227072 | tf_op jit(solution)/shard_map/all_gather | solution.py:108
  40.0 5.7 copy-start.19
  40.3 6.1 copy-start.25
  40.6 0.6 copy-start.30
  41.2 5.2 copy-start.37
  43.1 6.3 copy-start.13
  47.5 4.3 copy-start.9
  49.6 1.0 copy-start.1
  51.8 8.3 copy-start.16
  57.8 13.8 copy-start.3
  57.8 4.7 copy-start.28
  59.3 0.8 copy-start.5
  61.2 0.9 copy-start.2
  61.2 0.8 copy-start.23
  61.4 0.6 copy-start.32
  62.0 0.6 copy-start.29
  67.0 784.5 %reduce-scatter.2.cloned.1.call-start = ((), (), s32[]{:S(2)}) async-start(), calls=%async_computation.5 | async-start | bytes 8454144 | tf_op jit(solution)/shard_map/reduce_scatter | solution.py:125
  86.0 28.8 %copy-start.17 = (bf16[128,4,32]{2,1,0:T(4,128)(2,1)S(1)}, bf16[128,4,32]{2,1,0:T(4,128)(2,1)}, u32[]{:S(2)}) copy-start(bf16[128,4,32]{2,1,0:T(4,128)(2,1)} %get-tuple-element.13) | copy-start | bytes 98308
  132.6 28.5 %all-to-all-start = ((bf16[128,2,512]{2,1,0:T(2,128)(2,1)}), bf16[128,2,512]{2,1,0:T(2,128)(2,1)}, u32[]{:S(2)}, u32[]{:S(2)}) async-start(bf16[128,2,512]{2,1,0:T(2,128)(2,1)} %reshape.254), calls=%async_computation | async-start | bytes 524288 | tf_op jit(solution)/shard_map/all_to_all | solution.py:78
  139.2 17.6 copy-start.24
  139.2 18.7 copy-start.26
  139.2 19.4 %copy-start.40 = (f32[512]{0:T(512)S(1)}, f32[512]{0:T(512)}, u32[]{:S(2)}) copy-start(f32[512]{0:T(512)} %get-tuple-element.20) | copy-start | bytes 6148
  139.3 20.1 %copy-start.39 = (f32[512]{0:T(512)S(1)}, f32[512]{0:T(512)}, u32[]{:S(2)}) copy-start(f32[512]{0:T(512)} %get-tuple-element.18) | copy-start | bytes 6148
  139.3 20.8 %copy-start.11 = (f32[512,256]{1,0:T(8,128)S(1)}, f32[512,256]{1,0:T(8,128)}, u32[]{:S(2)}) copy-start(f32[512,256]{1,0:T(8,128)} %get-tuple-element.24) | copy-start | bytes 1572868
  139.3 1770.4 %all-reduce.3.cloned.1.call-start = ((), (), s32[]{:S(2)}) async-start(), calls=%async_computation.6 | async-start | bytes 1179648 | tf_op jit(solution)/shard_map/psum | solution.py:153
  163.4 122.6 %copy-start.8 = (bf16[512,1,256]{2,1,0:T(2,128)(2,1)}, bf16[512,1,256]{2,1,0:T(2,128)(2,1)S(1)}, u32[]{:S(2)}) copy-start(bf16[512,1,256]{2,1,0:T(2,128)(2,1)S(1)} %reshape.255) | copy-start | bytes 786436
  304.4 563.6 %copy-start.18 = (bf16[128,4,32]{0,2,1:T(8,128)(2,1)}, bf16[128,4,32]{0,2,1:T(8,128)(2,1)S(1)}, u32[]{:S(2)}) copy-start(bf16[128,4,32]{0,2,1:T(8,128)(2,1)S(1)} %fusion.26) | copy-start | bytes 98308
  852.3 15.7 copy-start.21
  854.5 0.6 copy-start.33
  857.1 2.7 copy-start.35
  865.3 4.4 copy-start.14
  869.6 1.4 copy-start.15
  871.0 1.2 copy-start.34
  875.4 14.5 copy-start.4
  875.4 14.5 copy-start.6
  876.8 14.4 copy-start.27
  880.7 9.2 copy-start.10
  880.7 12.7 copy-start.31
  882.7 10.9 copy-start.36
  882.7 13.3 copy-start.7
  889.9 9.8 copy-start.38
  891.2 9.0 copy-start.12
Sparse Core Ops, SparseCore 0:
  67.1 211.7 all-gather.1
  282.0 569.3 reduce-scatter.1
  900.3 1009.2 all-reduce.2
where the time goes:
time: 1930 us; the launch traced here: 1920 us
  waiting for transfers between devices  1640 us (85%)
  local copies, waits for them, and re-layouts  124 us (6%)
  matrix products  62.5 us (3%)
  blocking collectives  53.1 us (3%)
    psum x1, waiting for transfers between devices, body(): lax.psum((pair_update_gradient, tensor_mean_derivative), 'dap')  981 us
    reduce_scatter x1, waiting for transfers between devices, body(): lax.psum_scatter(jnp.einsum('sic,ijce->jse', left_factor, pair_grad, pref...  547 us
    all_gather x1, waiting for transfers between devices, body(): right_whole = lax.all_gather(right_factor, 'dap', axis=1, tiled=True)  112 us
    reshape x3, local copies, waits for them, and re-layouts, body(): pair_grad.reshape(residue_total, twofold_change_adjoint.shape[1], factor_...  54.2 us
  transfers between devices with their start and end apart: 4, of which 3 were waited for; matrix products, arithmetic and copies ran while one was open for 6% of the time, Pallas kernels for 0%

commit v1 on v0

v1 whole, which is shorter than its diff:
```python
import functools

import jax
import jax.numpy as jnp
from jax import lax
from jax.experimental import pallas as pl
from jax.experimental.pallas import tpu as pltpu
from jax.sharding import PartitionSpec as P

HEADS = 8
HEAD_DIM = 32
SEQ = 128
RES = 4
CH = 256
N_DAP = 128
N_WIDE = 16
N_Z = 8
MESH = pl.DeviceIdType.MESH
F32 = jnp.float32
BF16 = jnp.bfloat16


def nn(a, b):
    return lax.dot_general(a, b, (((1,), (0,)), ((), ())), preferred_element_type=F32)


def nt(a, b):
    return lax.dot_general(a, b, (((1,), (1,)), ((), ())), preferred_element_type=F32)


def peer_all(me, k):
    return lax.rem(me + k, N_DAP)


def peer_z(me, k):
    low = lax.rem(me, 16)
    return me - low + lax.rem(low + 2 * k, 16)


def peer_wide(me, k):
    core = lax.rem(me, 2)
    member = lax.rem((me // 16) * 2 + core + k, N_WIDE)
    return (member // 2) * 16 + lax.rem(me, 16) - core + lax.rem(member, 2)


def place_wide(me):
    return (me // 16) * 2 + lax.rem(me, 2)


def place_z(me):
    return lax.rem(me, 16) // 2


def push(peer_of, place_of, total, me, src, dst, send_sem, recv_sem, spread):
    mine = place_of(me)

    def one(k, carry):
        peer = peer_of(me, k)
        pltpu.make_async_remote_copy(
            src_ref=src.at[place_of(peer)] if spread else src,
            dst_ref=dst.at[mine],
            send_sem=send_sem,
            recv_sem=recv_sem,
            device_id={"dap": peer},
            device_id_type=MESH,
        ).start()
        return carry

    lax.fori_loop(1, total, one, 0)


def drain(ref, total, sem):
    part = ref.at[pl.ds(0, total - 1)]
    pltpu.make_async_copy(part, part, sem).wait()


def standardize(wide):
    average = jnp.mean(wide, axis=-1, keepdims=True)
    centred = wide - average
    variance = jnp.mean(centred * centred, axis=-1, keepdims=True)
    scale = lax.rsqrt(variance + 1e-05)
    return centred * scale, scale


def standardize_back(grad, hat, scale):
    return scale * (
        grad
        - jnp.mean(grad, axis=-1, keepdims=True)
        - hat * jnp.mean(grad * hat, axis=-1, keepdims=True)
    )


def kernel(
    rows_ref, wq_ref, wk_ref, wv_ref, wg_ref, shift_ref, wo_ref, wf_ref, wp_ref, adj_ref, pair_ref,
    out_ref, pwg_ref, owg_ref, rfg_ref,
    xs, xr, us, ur, gs, gr, t32, x32, hat_in, sc_in, gate, att, q_all, k_all, v_all, w_all,
    nmid, hat_mid, sc_mid, fac_t, ls, lg, rs, rg, lp, g2, w2, y, xp, pacc, gls, glr, grs, grr,
    dcat, ps, pr, zs, zr, fs, fr, os, orr, send, recv,
):
    me = lax.axis_index("dap")
    wide = place_wide(me)
    along = place_z(me)
    bar = pltpu.get_barrier_semaphore()

    def greet(k, carry):
        pl.semaphore_signal(bar, inc=1, device_id={"dap": peer_all(me, k)}, device_id_type=MESH)
        return carry

    lax.fori_loop(1, N_DAP, greet, 0)

    def stage_rows(ref, dst):
        t32[pl.ds(0, 512, stride=2), :] = ref[:, 0:128].astype(F32)
        t32[pl.ds(1, 512, stride=2), :] = ref[:, 128:256].astype(F32)
        dst[...] = t32[0:1024, :].reshape(N_DAP, 8, 128).astype(BF16)

    stage_rows(rows_ref, xs)
    g2[...] = jnp.zeros_like(g2)
    fac_t[...] = wf_ref[...].astype(F32).T.astype(BF16)
    for c_hi in range(16):
        for c_lo in range(2):
            w2[c_hi * 32:(c_hi + 1) * 32, c_lo * 128:(c_lo + 1) * 128] = (
                wp_ref[(2 * c_hi + c_lo) * 32:(2 * c_hi + c_lo + 1) * 32, :].astype(F32) * (1.0 / SEQ)
            ).astype(BF16)
    xr[me] = xs[me]
    pl.semaphore_wait(bar, N_DAP - 1)

    push(peer_all, lambda d: d, N_DAP, me, xs, xr, send.at[0], recv.at[0], True)

    t32[...] = pair_ref[...].astype(F32)

    def stage_pair(at, carry):
        for core in range(2):
            for i in range(RES):
                parts = [
                    t32[pl.ds(i * 512 + at * 64 + core * 4 + r, 8, stride=8), :] for r in range(RES)
                ]
                gs[at * 2 + core, i * 32:(i + 1) * 32, :] = jnp.concatenate(parts, axis=0).astype(BF16)
        return carry

    lax.fori_loop(0, 8, stage_pair, 0)
    gr[wide] = gs[wide]
    push(peer_wide, place_wide, N_WIDE, me, gs, gr, send.at[1], recv.at[1], True)
    stage_rows(adj_ref, us)
    ur[me] = us[me]

    drain(xr, N_DAP, recv.at[0])
    push(peer_all, lambda d: d, N_DAP, me, us, ur, send.at[2], recv.at[2], True)

    t32[0:1024, :] = xr[...].astype(F32).reshape(1024, 128)
    lane_head = lax.broadcasted_iota(jnp.int32, (1, CH), 1) // HEAD_DIM
    masks = [(lane_head == h).astype(F32).astype(BF16) for h in range(HEADS)]

    def blocks(value):
        return jnp.concatenate([value * m for m in masks], axis=0)

    def side_by_side(value):
        return jnp.concatenate([value[h * 128:(h + 1) * 128, :] for h in range(HEADS)], axis=1)

    def forward(r, carry):
        x = jnp.concatenate(
            [t32[pl.ds(2 * r + half, SEQ, stride=8), :] for half in range(2)], axis=1
        )
        x32[r] = x
        hat, scale = standardize(x)
        hat_in[r] = hat
        sc_in[r] = jnp.broadcast_to(scale, (SEQ, 128))
        normed = hat.astype(BF16)
        q = (nn(normed, wq_ref[...]) * HEAD_DIM ** (-0.5)).astype(BF16)
        k = nn(normed, wk_ref[...]).astype(BF16)
        v = nn(normed, wv_ref[...]).astype(BF16)
        g = jax.nn.sigmoid(nn(normed, wg_ref[...]) + shift_ref[...])
        q_all[r] = q
        k_all[r] = k
        v_all[r] = v
        gate[r] = g
        scores = nt(blocks(q), k)
        e = jnp.exp(scores - jnp.max(scores, axis=-1, keepdims=True))
        w = e * (1.0 / jnp.sum(e, axis=-1, keepdims=True))
        w_all[r] = w
        a = nn(side_by_side(w.astype(BF16)), blocks(v))
        att[r] = a
        gated = (a * g).astype(BF16)
        upd = (x + nn(gated, wo_ref[...])).astype(BF16).astype(F32)
        hat, scale = standardize(upd)
        hat_mid[r] = hat
        sc_mid[r] = jnp.broadcast_to(scale, (SEQ, 128))
        normed = hat.astype(BF16)
        nmid[r] = normed
        factors = nt(fac_t[...], normed).astype(BF16)
        at = pl.multiple_of(r * 32, 32)
        ls[pl.ds(at, 32), :] = factors[0:32, :]
        rs[pl.ds(at, 32), :] = factors[32:64, :]
        return carry

    lax.fori_loop(0, RES, forward, 0)

    push(peer_z, place_z, N_Z, me, rs, rg, send.at[3], recv.at[3], False)
    push(peer_wide, place_wide, N_WIDE, me, ls, lg, send.at[4], recv.at[4], False)
    rg[along] = rs[...]
    lg[wide] = ls[...]

    drain(gr, N_WIDE, recv.at[1])
    t32[...] = gr[...].astype(F32).reshape(2048, 128)

    def build(jn, carry):
        jp = lax.rem(jn, 4) * 8 + jn // 4
        part = jnp.concatenate(
            [t32[pl.ds(r * 32 + jp, 16, stride=128), :] for r in range(RES)], axis=0
        ).astype(BF16)
        g2[jn, 0:64, 0:128] = part
        g2[jn, 64:128, 128:256] = part
        return carry

    lax.fori_loop(0, 32, build, 0)

    def pair_grad(at, carry):
        res = nt(w2[...], g2[pl.ds(at * 4, 4)].reshape(512, 256)).astype(BF16)
        for jj in range(4):
            for c_hi in range(16):
                y[at * 4 + jj, :, c_hi * 128:(c_hi + 1) * 128] = res[
                    c_hi * 32:(c_hi + 1) * 32, jj * 128:(jj + 1) * 128
                ]
        return carry

    lax.fori_loop(0, 8, pair_grad, 0)

    drain(lg, N_WIDE, recv.at[4])
    t32[...] = lg[...].astype(F32).reshape(2048, 128)

    def order_left(c, carry):
        part = jnp.concatenate(
            [t32[pl.ds(r * 32 + c, 16, stride=128), :] for r in range(RES)], axis=0
        )
        lp[pl.ds(pl.multiple_of(c * 64, 64), 64), :] = part.astype(BF16)
        return carry

    lax.fori_loop(0, 32, order_left, 0)

    def right_grad(at, carry):
        res = nn(y[pl.ds(at * 8, 8)].reshape(256, 2048), lp[...]).astype(BF16)
        grs[pl.ds(at * 2, 2)] = res.reshape(2, 128, 128)
        return carry

    lax.fori_loop(0, 4, right_grad, 0)
    grr[along] = grs[along]
    push(peer_z, place_z, N_Z, me, grs, grr, send.at[5], recv.at[5], True)

    drain(rg, N_Z, recv.at[3])
    rg_t = rg[...].reshape(1024, 128).astype(F32).T.astype(BF16)

    def left_grad(at, carry):
        col = pl.multiple_of(at * 512, 512)
        res = nn(rg_t, y[:, :, pl.ds(col, 512)].reshape(1024, 512))
        t32[pl.ds(col, 512), :] = res.T
        return carry

    lax.fori_loop(0, 4, left_grad, 0)

    def stage_left(m, carry):
        part = jnp.concatenate(
            [t32[pl.ds(m + 16 * r, 32, stride=64), :] for r in range(RES)], axis=0
        )
        gls[m] = part.astype(BF16)
        return carry

    lax.fori_loop(0, 16, stage_left, 0)
    glr[wide] = gls[wide]
    push(peer_wide, place_wide, N_WIDE, me, gls, glr, send.at[6], recv.at[6], True)

    pacc[...] = jnp.zeros_like(pacc)

    def pair_weight(at, carry):
        rows = rg[pl.ds(at * 2, 2)].reshape(256, 128)
        for group in range(4):
            res = nt(rows, lp[group * 512:(group + 1) * 512, :]).astype(BF16)
            for jj in range(8):
                for cc in range(4):
                    c_hi = group * 4 + cc
                    xp[c_hi * 32:(c_hi + 1) * 32, jj * 128:(jj + 1) * 128] = res[
                        jj * 32:(jj + 1) * 32, cc * 128:(cc + 1) * 128
                    ]
        pacc[...] += nn(xp[...], g2[pl.ds(at * 8, 8)].reshape(1024, 256))
        return carry

    lax.fori_loop(0, 4, pair_weight, 0)

    drain(grr, N_Z, recv.at[5])
    right_sum = jnp.sum(grr[...].astype(F32), axis=0)
    drain(glr, N_WIDE, recv.at[6])
    left_sum = jnp.sum(glr[...].astype(F32), axis=0)
    rfg_ref[...] = right_sum.T
    owg = jnp.zeros((64, CH), F32)
    for r in range(RES):
        both = jnp.concatenate(
            [left_sum[r * 32:(r + 1) * 32, :], right_sum[r * 32:(r + 1) * 32, :]], axis=0
        )
        owg = owg + nn(both.astype(BF16), nmid[r])
        dcat[r] = both.T.astype(BF16)

    for m in range(16):
        part = pacc[m * 32:(m + 1) * 32, :] * (1.0 / SEQ)
        half = m // 8
        ps[m] = jnp.concatenate(
            [
                part[:, 0:128],
                part[:, 128:256],
                owg[(m % 8) * 8:(m % 8) * 8 + 8, half * 128:(half + 1) * 128],
                jnp.zeros((8, 128), F32),
            ],
            axis=0,
        ).astype(BF16)
    pr[wide] = ps[wide]
    push(peer_wide, place_wide, N_WIDE, me, ps, pr, send.at[7], recv.at[7], True)

    drain(ur, N_DAP, recv.at[2])
    t32[1024:2048, :] = ur[...].astype(F32).reshape(1024, 128)

    def backward(r, carry):
        grad = nn(dcat[r], fac_t[...]).astype(BF16).astype(F32)
        dmid = standardize_back(grad, hat_mid[r], sc_mid[r][:, 0:1]).astype(BF16).astype(F32)
        arriving = jnp.concatenate(
            [t32[pl.ds(1024 + 2 * r + half, SEQ, stride=8), :] for half in range(2)], axis=1
        )
        gm16 = (arriving + dmid).astype(BF16)
        gm = gm16.astype(F32)
        dgated = nt(gm16, wo_ref[...]).astype(BF16).astype(F32)
        g = gate[r]
        datt = blocks((dgated * g).astype(BF16))
        dpre = (dgated * att[r] * g * (1.0 - g)).astype(BF16)
        w = w_all[r]
        dw = nt(datt, v_all[r])
        ds = w * (dw - jnp.sum(w * dw, axis=-1, keepdims=True))
        dq = nn(side_by_side(ds.astype(BF16)), blocks(k_all[r])).astype(BF16)
        dq = (dq.astype(F32) * HEAD_DIM ** (-0.5)).astype(BF16)
        dk = nn(ds.T.astype(BF16), blocks(q_all[r])).astype(BF16)
        dv = nn(w.T.astype(BF16), datt).astype(BF16)
        dnorm = (
            nt(dq, wq_ref[...]) + nt(dk, wk_ref[...]) + nt(dv, wv_ref[...]) + nt(dpre, wg_ref[...])
        ).astype(BF16).astype(F32)
        dx = standardize_back(dnorm, hat_in[r], sc_in[r][:, 0:1]).astype(BF16).astype(F32)
        total = gm + dx
        for half in range(2):
            t32[pl.ds(2 * r + half, SEQ, stride=8), :] = total[:, half * 128:(half + 1) * 128]
        return carry

    lax.fori_loop(0, 2, backward, 0)

    drain(pr, N_WIDE, recv.at[7])
    zs[...] = jnp.sum(pr[...].astype(F32), axis=0).astype(BF16)
    zr[along] = zs[...]
    push(peer_z, place_z, N_Z, me, zs, zr, send.at[8], recv.at[8], False)

    lax.fori_loop(2, RES, backward, 0)

    os[...] = t32[0:1024, :].reshape(N_DAP, 8, 128).astype(BF16)
    orr[me] = os[me]
    push(peer_all, lambda d: d, N_DAP, me, os, orr, send.at[10], recv.at[10], True)

    drain(zr, N_Z, recv.at[8])
    fs[...] = jnp.sum(zr[...].astype(F32), axis=0).astype(BF16)
    fr[wide] = fs[...]
    push(peer_wide, place_wide, N_WIDE, me, fs, fr, send.at[9], recv.at[9], False)
    drain(xs, N_DAP, send.at[0])
    drain(gs, N_WIDE, send.at[1])
    drain(us, N_DAP, send.at[2])
    drain(rg, N_Z, send.at[3])
    drain(lg, N_WIDE, send.at[4])
    drain(grs, N_Z, send.at[5])
    drain(gls, N_WIDE, send.at[6])
    drain(ps, N_WIDE, send.at[7])
    drain(zr, N_Z, send.at[8])
    drain(fr, N_WIDE, send.at[9])
    drain(fr, N_WIDE, recv.at[9])
    halves = []
    for m in range(16):
        pwg_ref[m * 64:(m + 1) * 64, :] = fr[m, 0:64, :].astype(F32)
        halves.append(fr[m, 64:80, :].astype(F32)[0:8, :])
    owg_t = jnp.concatenate(
        [jnp.concatenate(halves[0:8], axis=0), jnp.concatenate(halves[8:16], axis=0)], axis=1
    )
    owg_ref[...] = owg_t.T

    drain(os, N_DAP, send.at[10])
    drain(orr, N_DAP, recv.at[10])
    t32[0:1024, :] = orr[...].astype(F32).reshape(1024, 128)
    out_ref[:, 0:128] = t32[pl.ds(0, 512, stride=2), :].astype(BF16)
    out_ref[:, 128:256] = t32[pl.ds(1, 512, stride=2), :].astype(BF16)


SCRATCH = (
    [((N_DAP, 8, 128), BF16)] * 4
    + [((16, 128, 128), BF16)] * 2
    + [((2048, 128), F32)]
    + [((RES, SEQ, CH), F32)] * 2
    + [((RES, SEQ, 128), F32)]
    + [((RES, SEQ, CH), F32)] * 2
    + [((RES, SEQ, CH), BF16)] * 3
    + [((RES, HEADS * SEQ, SEQ), F32)]
    + [((RES, SEQ, CH), BF16)]
    + [((RES, SEQ, CH), F32)]
    + [((RES, SEQ, 128), F32)]
    + [((64, CH), BF16)]
    + [((128, 128), BF16), ((16, 128, 128), BF16)]
    + [((128, 128), BF16), ((8, 128, 128), BF16)]
    + [((2048, 128), BF16)]
    + [((32, 128, 256), BF16)]
    + [((512, 256), BF16)]
    + [((32, 32, 2048), BF16)]
    + [((512, 1024), BF16)]
    + [((512, 256), F32)]
    + [((16, 128, 128), BF16)] * 2
    + [((8, 128, 128), BF16)] * 2
    + [((RES, SEQ, 64), BF16)]
    + [((16, 80, 128), BF16)] * 2
    + [((80, 128), BF16), ((8, 80, 128), BF16)]
    + [((80, 128), BF16), ((16, 80, 128), BF16)]
    + [((N_DAP, 8, 128), BF16)] * 2
)


def body(
    aligned_rows,
    asking_projection,
    lookup_projection,
    content_projection,
    sigmoid_projection,
    sigmoid_shift,
    result_projection,
    tensor_mean_projections,
    twofold_projection,
    refreshed_rows_adjoint,
    twofold_change_adjoint,
):
    whole = pl.BlockSpec(memory_space=pltpu.VMEM)
    out, pwg, owg, rfg = pl.pallas_call(
        kernel,
        out_shape=(
            jax.ShapeDtypeStruct((512, CH), BF16),
            jax.ShapeDtypeStruct((1024, 128), F32),
            jax.ShapeDtypeStruct((CH, 64), F32),
            jax.ShapeDtypeStruct((SEQ, 128), F32),
        ),
        in_specs=[whole] * 11,
        out_specs=(whole,) * 4,
        scratch_shapes=[pltpu.VMEM(shape, kind) for shape, kind in SCRATCH]
        + [pltpu.SemaphoreType.DMA((11,)), pltpu.SemaphoreType.DMA((11,))],
        compiler_params=pltpu.CompilerParams(
            collective_id=0, has_side_effects=True, vmem_limit_bytes=56 * 2**20
        ),
        name="evoformer_backward",
    )(
        aligned_rows.reshape(512, CH),
        asking_projection,
        lookup_projection,
        content_projection,
        sigmoid_projection,
        sigmoid_shift.reshape(1, CH),
        result_projection,
        tensor_mean_projections,
        twofold_projection,
        refreshed_rows_adjoint.reshape(512, CH),
        twofold_change_adjoint.reshape(2048, 128),
    )
    return (out.reshape(1, 512, CH), pwg, owg, rfg.reshape(SEQ, RES, 32))


def solution(mesh):
    split = P(("dp", "dap"), None, None)
    in_specs = (split,) + (P(),) * 8 + (split, split)
    out_specs = (split, P("dp", None), P("dp", None), P("dp", "dap", None))
    return jax.shard_map(body, mesh=mesh, in_specs=in_specs, out_specs=out_specs, check_vma=False)
```

time: 1930 us -> 84.4 us (0.04)
  waiting for transfers between devices: 1640 us -> 0 us
  local copies, waits for them, and re-layouts: 124 us -> 7.2 us
  Pallas kernels: 0 us -> 76.2 us
  matrix products: 62.5 us -> 0 us
  blocking collectives: 53.1 us -> 0 us
    psum x1 -> x0, waiting for transfers between devices: 981 us -> none  [body(): lax.psum((pair_update_gradient, tensor_mean_derivative), 'dap')]
    reduce_scatter x1 -> x0, waiting for transfers between devices: 547 us -> none  [body(): lax.psum_scatter(jnp.einsum('sic,ijce->jse', left_factor, pair_grad, pref...]
    all_gather x1 -> x0, waiting for transfers between devices: 112 us -> none  [body(): right_whole = lax.all_gather(right_factor, 'dap', axis=1, tiled=True)]
    pallas_call x0 -> x1, Pallas kernels: none -> 76.2 us  [body(): pl.pallas_call(kernel, out_shape=(jax.ShapeDtypeStruct((512, CH), BF16),...]
    reshape x14 -> x0, local copies, waits for them, and re-layouts: 68 us -> none  [the longest x3 54.2 us: body(): pair_grad.reshape(residue_total, twofold_change_adjoint.shape[1], factor_...]
    dot_general x23 -> x0, matrix products: 60.7 us -> none  [the longest x1 11.7 us: body(): jnp.einsum('ijce,sje->sic', pair_grad, right_whole, preferred_element_typ...]
    all_to_all x2 -> x0, blocking collectives: 53.1 us -> none  [the longest x1 28.3 us: body(): lax.all_to_all(aligned_rows, 'dap', split_axis=1, concat_axis=0, tiled=True)]
  transfers between devices with their start and end apart: 4 -> 0, of which waited for: 3 -> 0; matrix products, arithmetic and copies ran while one was open for 6% -> 0% of each run, Pallas kernels for 0% -> 0%
where the time goes in v1:
time: 84.4 us; the launch traced here: 84.1 us
  Pallas kernels  76.2 us (90%)
  local copies, waits for them, and re-layouts  7.2 us (9%)
    pallas_call x1, Pallas kernels, body(): pl.pallas_call(kernel, out_shape=(jax.ShapeDtypeStruct((512, CH), BF16),...  76.2 us
    unnamed x6, local copies, waits for them, and re-layouts  5.63 us

profile of v1, /device:TPU:1, one launch (start us, length us, event | category | flops | bytes accessed | tf_op | source)
XLA Modules:
  0.0 84.1 jit_solution(13996244987204423052)
XLA Ops:
  0.6 1.5 %copy.18.wf_ref = bf16[256,64]{1,0:T(8,128)(2,1)} copy(bf16[256,64]{0,1:T(8,128)(2,1)} %param.18) | data formatting | bytes 65536 | tf_op args[7]
  2.1 76.2 %evoformer_backward.1 = (bf16[512,256]{1,0:T(8,128)(2,1)}, f32[1024,128]{1,0:T(8,128)}, f32[256,64]{1,0:T(8,128)}, f32[128,128]{1,0:T(8,128)}) custom-call(bf16[512,256]{1,0:T(8,128)(2,1)} %bitcast.7, bf16[256,256]{1,0:T(8,128)(2,1)} %wq_ref.1, bf16[256,256]{1,0:T(8,128)(2,1)} %wk_ref.1, bf16[256,256]{1,0:T(8,128)(2,1)} %wv_ref.1, bf16[256,256]{1,0:T(8,128)(2,1)} %wg_ref.1, ...), custom_call_target="tpu_custom_call" | custom-call | tf_op jit(solution)/shard_map/evoformer_backward/pallas_call | solution.py:435
  78.4 0.0 copy-start
  78.4 1.7 %copy.20 = f32[256,64]{0,1:T(8,128)} copy(f32[256,64]{1,0:T(8,128)} %get-tuple-element.18) | data formatting | bytes 131072
  80.0 1.6 %copy.19 = f32[128,128]{0,1:T(8,128)} copy(f32[128,128]{1,0:T(8,128)} %get-tuple-element.11) | data formatting | bytes 131072 | tf_op jit(solution)/shard_map/evoformer_backward/pallas_call | solution.py:435
  81.6 1.7 %copy.23 = bf16[1,512,256]{2,1,0:T(8,128)(2,1)} copy(bf16[1,512,256]{2,1,0:T(8,128)(2,1)} %bitcast.9) | data formatting | bytes 524288
  83.3 0.0 copy-done
  83.3 0.8 copy.24
Async XLA Ops:
  78.4 4.9 %copy-start = (f32[1024,128]{1,0:T(8,128)S(1)}, f32[1024,128]{1,0:T(8,128)}, u32[]{:S(2)}) copy-start(f32[1024,128]{1,0:T(8,128)} %get-tuple-element.25) | copy-start | bytes 1572868

commit v2 on v1

v2 whole, which is shorter than its diff:
```python
import functools

import jax
import jax.numpy as jnp
from jax import lax
from jax.experimental import pallas as pl
from jax.experimental.pallas import tpu as pltpu
from jax.sharding import PartitionSpec as P

HEADS = 8
HEAD_DIM = 32
SEQ = 128
RES = 4
CH = 256
N_DAP = 128
N_WIDE = 16
N_Z = 8
MESH = pl.DeviceIdType.MESH
F32 = jnp.float32
BF16 = jnp.bfloat16


def nn(a, b):
    return lax.dot_general(a, b, (((1,), (0,)), ((), ())), preferred_element_type=F32)


def nt(a, b):
    return lax.dot_general(a, b, (((1,), (1,)), ((), ())), preferred_element_type=F32)


def far_first():
    steps = [
        (dx, dy, dz, dc)
        for dy in range(4) for dz in range(8) for dx in range(2) for dc in range(2)
        if dx or dy or dz or dc
    ]
    return sorted(steps, key=lambda d: -(2 * (d[0] + min(d[1], 4 - d[1]) + min(d[2], 8 - d[2])) + d[3]))


def groups(me):
    x = lax.div(me, 64)
    y = lax.rem(lax.div(me, 16), 4)
    z = lax.rem(lax.div(me, 2), 8)
    core = lax.rem(me, 2)
    step = 1 - 2 * core
    xs = [x * 64, (1 - x) * 64]
    ys = [lax.rem(y + 4 + d * step, 4) * 16 for d in range(4)]
    zs = [lax.rem(z + 8 + d * step, 8) for d in range(8)]
    twice = [place * 2 for place in zs]
    cores = [core, 1 - core]
    everyone = []
    for dx, dy, dz, dc in far_first():
        device = xs[dx] + ys[dy] + twice[dz] + cores[dc]
        everyone.append((device, device))
    wide = []
    for dx, dy, dc in (
        (1, 2, 0), (0, 2, 1), (1, 1, 0), (1, 3, 1), (1, 2, 1), (0, 2, 0), (1, 1, 1), (1, 3, 0),
        (0, 1, 0), (0, 3, 1), (1, 0, 0), (0, 1, 1), (0, 3, 0), (1, 0, 1), (0, 0, 1),
    ):
        line = xs[dx] + ys[dy]
        wide.append((line + z * 2 + cores[dc], lax.div(line, 8) + cores[dc]))
    long = [(xs[0] + ys[0] + twice[dz] + core, zs[dz]) for dz in (4, 3, 5, 2, 6, 1, 7)]
    return (me, everyone), (lax.div(xs[0] + ys[0], 8) + core, wide), (z, long)


def push(group, src, dst, send_sem, recv_sem, spread):
    mine, others = group
    for device, place in others:
        pltpu.make_async_remote_copy(
            src_ref=src.at[place] if spread else src,
            dst_ref=dst.at[mine],
            send_sem=send_sem,
            recv_sem=recv_sem,
            device_id={"dap": device},
            device_id_type=MESH,
        ).start()


def drain(ref, total, sem):
    part = ref.at[pl.ds(0, total - 1)]
    pltpu.make_async_copy(part, part, sem).wait()


def standardize(wide):
    average = jnp.mean(wide, axis=-1, keepdims=True)
    centred = wide - average
    variance = jnp.mean(centred * centred, axis=-1, keepdims=True)
    scale = lax.rsqrt(variance + 1e-05)
    return centred * scale, scale


def standardize_back(grad, hat, scale):
    return scale * (
        grad
        - jnp.mean(grad, axis=-1, keepdims=True)
        - hat * jnp.mean(grad * hat, axis=-1, keepdims=True)
    )


def kernel(
    rows_ref, wq_ref, wk_ref, wv_ref, wg_ref, shift_ref, wo_ref, wf_ref, wp_ref, adj_ref, pair_ref,
    out_ref, pwg_ref, owg_ref, rfg_ref,
    xs, xr, us, ur, gs, gr, t32, u32, hat_in, sc_in, gate, att, q_all, k_all,
    v_all, w_all, nmid, hat_mid, sc_mid, ls, lg, rs, rg, lp, g2, w2, y, xp, pacc, gls, glr, grs, grr,
    dcat, ps, pr, qs, qr, zs, zr, fs, fr, os, orr, send, recv,
):
    me = lax.axis_index("dap")
    whole_group, wide_group, long_group = groups(me)
    wide, along = wide_group[0], long_group[0]
    bar = pltpu.get_barrier_semaphore()
    for device, _ in whole_group[1]:
        pl.semaphore_signal(bar, inc=1, device_id={"dap": device}, device_id_type=MESH)

    def push_all(src, dst, sem):
        push(whole_group, src, dst, send.at[sem], recv.at[sem], True)

    def push_wide(src, dst, sem, spread):
        push(wide_group, src, dst, send.at[sem], recv.at[sem], spread)

    def push_z(src, dst, sem, spread):
        push(long_group, src, dst, send.at[sem], recv.at[sem], spread)

    def stage_rows(ref, dst):
        u32[pl.ds(0, 512, stride=2), :] = ref[:, 0:128].astype(F32)
        u32[pl.ds(1, 512, stride=2), :] = ref[:, 128:256].astype(F32)
        dst[...] = u32[...].reshape(N_DAP, 8, 128).astype(BF16)

    stage_rows(rows_ref, xs)
    xr[me] = xs[me]
    pl.semaphore_wait(bar, N_DAP - 1)

    push_all(xs, xr, 0)

    t32[...] = pair_ref[...].astype(F32)

    def stage_pair(at, carry):
        for core in range(2):
            for i in range(RES):
                parts = [
                    t32[pl.ds(i * 512 + at * 64 + core * 4 + r, 8, stride=8), :] for r in range(RES)
                ]
                gs[at * 2 + core, i * 32:(i + 1) * 32, :] = jnp.concatenate(parts, axis=0).astype(BF16)
        return carry

    lax.fori_loop(0, 8, stage_pair, 0)
    gr[wide] = gs[wide]
    push_wide(gs, gr, 8, True)

    stage_rows(adj_ref, us)
    ur[me] = us[me]
    g2[...] = jnp.zeros_like(g2)
    for c_hi in range(16):
        for c_lo in range(2):
            w2[c_hi * 32:(c_hi + 1) * 32, c_lo * 128:(c_lo + 1) * 128] = (
                wp_ref[(2 * c_hi + c_lo) * 32:(2 * c_hi + c_lo + 1) * 32, :].astype(F32) * (1.0 / SEQ)
            ).astype(BF16)

    drain(xr, N_DAP, recv.at[0])
    u32[...] = xr[...].astype(F32).reshape(1024, 128)

    lane_head = lax.broadcasted_iota(jnp.int32, (1, CH), 1) // HEAD_DIM
    masks = [(lane_head == h).astype(F32).astype(BF16) for h in range(HEADS)]

    def blocks(value):
        return jnp.concatenate([value * m for m in masks], axis=0)

    def side_by_side(value):
        return jnp.concatenate([value[h * 128:(h + 1) * 128, :] for h in range(HEADS)], axis=1)

    def forward(r, carry):
        x = jnp.concatenate(
            [u32[pl.ds(2 * r + half, SEQ, stride=8), :] for half in range(2)], axis=1
        )
        hat, scale = standardize(x)
        hat_in[r] = hat
        sc_in[r] = jnp.broadcast_to(scale, (SEQ, 128))
        normed = hat.astype(BF16)
        q = (nn(normed, wq_ref[...]) * HEAD_DIM ** (-0.5)).astype(BF16)
        k = nn(normed, wk_ref[...]).astype(BF16)
        v = nn(normed, wv_ref[...]).astype(BF16)
        g = jax.nn.sigmoid(nn(normed, wg_ref[...]) + shift_ref[...])
        q_all[r] = q
        k_all[r] = k
        v_all[r] = v
        gate[r] = g
        scores = nt(blocks(q), k)
        e = jnp.exp(scores - jnp.max(scores, axis=-1, keepdims=True))
        w = e * (1.0 / jnp.sum(e, axis=-1, keepdims=True))
        w_all[r] = w
        a = nn(side_by_side(w.astype(BF16)), blocks(v))
        att[r] = a
        gated = (a * g).astype(BF16)
        upd = (x + nn(gated, wo_ref[...])).astype(BF16).astype(F32)
        hat, scale = standardize(upd)
        hat_mid[r] = hat
        sc_mid[r] = jnp.broadcast_to(scale, (SEQ, 128))
        normed = hat.astype(BF16)
        nmid[r] = normed
        factors = nt(wf_ref[...], normed).astype(BF16)
        ls[r] = factors[0:32, :]
        rs[r] = factors[32:64, :]
        push_wide(ls.at[r], lg.at[r], 11 + r, False)
        push_z(rs.at[r], rg.at[r], 15 + r, False)
        lg[r, wide] = ls[r]
        rg[r, along] = rs[r]
        return carry

    lax.fori_loop(0, RES, forward, 0)

    push_all(us, ur, 1)

    drain(gr, N_WIDE, recv.at[8])
    t32[...] = gr[...].astype(F32).reshape(2048, 128)

    def build(jn, carry):
        part = jnp.concatenate(
            [t32[pl.ds(r * 32 + jn, 16, stride=128), :] for r in range(RES)], axis=0
        ).astype(BF16)
        g2[jn, 0:64, 0:128] = part
        g2[jn, 64:128, 128:256] = part
        return carry

    lax.fori_loop(0, 32, build, 0)

    def pair_grad(at, carry):
        res = nt(w2[...], g2[pl.ds(at * 4, 4)].reshape(512, 256)).astype(BF16)
        for jj in range(4):
            for c_hi in range(16):
                y[at * 4 + jj, :, c_hi * 128:(c_hi + 1) * 128] = res[
                    c_hi * 32:(c_hi + 1) * 32, jj * 128:(jj + 1) * 128
                ]
        return carry

    lax.fori_loop(0, 8, pair_grad, 0)

    for r in range(RES):
        drain(lg.at[r], N_WIDE, recv.at[11 + r])
    t32[...] = lg[...].astype(F32).reshape(2048, 128)

    def order_left(c, carry):
        part = jnp.concatenate(
            [t32[pl.ds(r * 512 + c, 16, stride=32), :] for r in range(RES)], axis=0
        )
        lp[pl.ds(pl.multiple_of(c * 64, 64), 64), :] = part.astype(BF16)
        return carry

    lax.fori_loop(0, 32, order_left, 0)

    for r in range(RES):
        drain(rg.at[r], N_Z, recv.at[15 + r])
    rg_t = rg[...].reshape(1024, 128).astype(F32).T.astype(BF16)

    def left_grad(at, carry):
        col = pl.multiple_of(at * 512, 512)
        res = nn(rg_t, y[:, :, pl.ds(col, 512)].reshape(1024, 512))
        t32[0:512, :] = res.T
        for m in range(16):
            gls[at, m] = jnp.concatenate(
                [t32[pl.ds(m + 16 * r, 8, stride=64), :] for r in range(RES)], axis=0
            ).astype(BF16)
        glr[at, wide] = gls[at, wide]
        push_wide(gls.at[at], glr.at[at], 23 + at, True)
        return carry

    lax.fori_loop(0, 4, left_grad, 0)

    def right_grad(r, carry):
        res = nn(y[pl.ds(r * 8, 8)].reshape(256, 2048), lp[...]).astype(BF16)
        grs[r] = res.reshape(8, 32, 128)
        grr[r, along] = grs[r, along]
        push_z(grs.at[r], grr.at[r], 19 + r, True)
        return carry

    lax.fori_loop(0, RES, right_grad, 0)

    pacc[...] = jnp.zeros_like(pacc)

    def pair_weight(r, carry):
        rows = rg[r].reshape(256, 128)
        for group in range(4):
            res = nt(rows, lp[group * 512:(group + 1) * 512, :]).astype(BF16)
            for jj in range(8):
                for cc in range(4):
                    c_hi = group * 4 + cc
                    xp[c_hi * 32:(c_hi + 1) * 32, jj * 128:(jj + 1) * 128] = res[
                        jj * 32:(jj + 1) * 32, cc * 128:(cc + 1) * 128
                    ]
        pacc[...] += nn(xp[...], g2[pl.ds(r * 8, 8)].reshape(1024, 256))
        return carry

    lax.fori_loop(0, RES, pair_weight, 0)

    for m in range(16):
        part = pacc[m * 32:(m + 1) * 32, :] * (1.0 / SEQ)
        ps[m] = jnp.concatenate([part[:, 0:128], part[:, 128:256]], axis=0).astype(BF16)
    pr[wide] = ps[wide]
    push_wide(ps, pr, 27, True)

    for r in range(RES):
        drain(grr.at[r], N_Z, recv.at[19 + r])
    right_sum = jnp.sum(grr[...].astype(F32), axis=1)
    for at in range(4):
        drain(glr.at[at], N_WIDE, recv.at[23 + at])
    left_sum = jnp.sum(glr[...].astype(F32), axis=1)
    owg = jnp.zeros((64, CH), F32)
    for r in range(RES):
        both = jnp.concatenate(
            [left_sum[at, r * 8:(r + 1) * 8, :] for at in range(4)] + [right_sum[r]], axis=0
        )
        owg = owg + nn(both.astype(BF16), nmid[r])
        dcat[r] = both.T.astype(BF16)

    for m in range(16):
        half = m // 8
        qs[m] = jnp.concatenate(
            [
                owg[(m % 8) * 8:(m % 8) * 8 + 8, half * 128:(half + 1) * 128],
                jnp.zeros((8, 128), F32),
            ],
            axis=0,
        ).astype(BF16)
    qr[wide] = qs[wide]
    push_wide(qs, qr, 38, True)

    drain(ur, N_DAP, recv.at[1])
    t32[1024:2048, :] = ur[...].astype(F32).reshape(1024, 128)

    def backward(r, carry):
        grad = nn(dcat[r], wf_ref[...]).astype(BF16).astype(F32)
        dmid = standardize_back(grad, hat_mid[r], sc_mid[r][:, 0:1]).astype(BF16).astype(F32)
        arriving = jnp.concatenate(
            [t32[pl.ds(1024 + 2 * r + half, SEQ, stride=8), :] for half in range(2)], axis=1
        )
        gm16 = (arriving + dmid).astype(BF16)
        gm = gm16.astype(F32)
        dgated = nt(gm16, wo_ref[...]).astype(BF16).astype(F32)
        g = gate[r]
        datt = blocks((dgated * g).astype(BF16))
        dpre = (dgated * att[r] * g * (1.0 - g)).astype(BF16)
        w = w_all[r]
        dw = nt(datt, v_all[r])
        ds = w * (dw - jnp.sum(w * dw, axis=-1, keepdims=True))
        dq = nn(side_by_side(ds.astype(BF16)), blocks(k_all[r])).astype(BF16)
        dq = (dq.astype(F32) * HEAD_DIM ** (-0.5)).astype(BF16)
        dk = nn(ds.T.astype(BF16), blocks(q_all[r])).astype(BF16)
        dv = nn(w.T.astype(BF16), datt).astype(BF16)
        dnorm = (
            nt(dq, wq_ref[...]) + nt(dk, wk_ref[...]) + nt(dv, wv_ref[...]) + nt(dpre, wg_ref[...])
        ).astype(BF16).astype(F32)
        dx = standardize_back(dnorm, hat_in[r], sc_in[r][:, 0:1]).astype(BF16).astype(F32)
        total = gm + dx
        for half in range(2):
            u32[pl.ds(2 * r + half, SEQ, stride=8), :] = total[:, half * 128:(half + 1) * 128]
        return carry

    lax.fori_loop(0, 2, backward, 0)

    drain(pr, N_WIDE, recv.at[27])
    drain(qr, N_WIDE, recv.at[38])
    zs[0:64, :] = jnp.sum(pr[...].astype(F32), axis=0).astype(BF16)
    zs[64:80, :] = jnp.sum(qr[...].astype(F32), axis=0).astype(BF16)
    zr[along] = zs[...]
    push_z(zs, zr, 28, False)

    lax.fori_loop(2, RES, backward, 0)

    os[...] = u32[...].reshape(N_DAP, 8, 128).astype(BF16)
    orr[me] = os[me]
    push_all(os, orr, 2)
    drain(zr, N_Z, recv.at[28])
    fs[...] = jnp.sum(zr[...].astype(F32), axis=0).astype(BF16)
    fr[wide] = fs[...]
    push_wide(fs, fr, 29, False)

    rfg_ref[...] = right_sum.reshape(128, SEQ)
    drain(xr, N_DAP, send.at[0])
    drain(ur, N_DAP, send.at[1])
    for r in range(RES):
        drain(lg.at[r], N_WIDE, send.at[11 + r])
        drain(rg.at[r], N_Z, send.at[15 + r])
        drain(grr.at[r], N_Z, send.at[19 + r])
        drain(glr.at[r], N_WIDE, send.at[23 + r])
    drain(gr, N_WIDE, send.at[8])
    drain(pr, N_WIDE, send.at[27])
    drain(qr, N_WIDE, send.at[38])
    drain(zr, N_Z, send.at[28])

    drain(fr, N_WIDE, recv.at[29])
    halves = []
    for m in range(16):
        pwg_ref[m * 64:(m + 1) * 64, :] = fr[m, 0:64, :].astype(F32)
        halves.append(fr[m, 64:80, :].astype(F32)[0:8, :])
    owg_ref[...] = jnp.concatenate(
        [jnp.concatenate(halves[0:8], axis=0), jnp.concatenate(halves[8:16], axis=0)], axis=1
    )
    drain(fr, N_WIDE, send.at[29])

    drain(orr, N_DAP, recv.at[2])
    u32[...] = orr[...].astype(F32).reshape(1024, 128)
    out_ref[:, 0:128] = u32[pl.ds(0, 512, stride=2), :].astype(BF16)
    out_ref[:, 128:256] = u32[pl.ds(1, 512, stride=2), :].astype(BF16)
    drain(orr, N_DAP, send.at[2])


def settle(*refs):
    found, results, held, arrive, leave = refs[0:4], refs[4:8], refs[8:12], refs[12], refs[13]
    ins = [pltpu.make_async_copy(found[n], held[n], arrive.at[n]) for n in range(4)]
    outs = [pltpu.make_async_copy(held[n], results[n], leave.at[n]) for n in range(4)]
    for copy in ins:
        copy.start()
    for n in range(4):
        ins[n].wait()
        outs[n].start()
    for copy in outs:
        copy.wait()


SCRATCH = (
    [((N_DAP, 8, 128), BF16)] * 4
    + [((16, 128, 128), BF16)] * 2
    + [((2048, 128), F32), ((1024, 128), F32)]
    + [((RES, SEQ, CH), F32)]
    + [((RES, SEQ, 128), F32)]
    + [((RES, SEQ, CH), F32)] * 2
    + [((RES, SEQ, CH), BF16)] * 3
    + [((RES, HEADS * SEQ, SEQ), F32)]
    + [((RES, SEQ, CH), BF16)]
    + [((RES, SEQ, CH), F32)]
    + [((RES, SEQ, 128), F32)]
    + [((RES, 32, 128), BF16), ((RES, 16, 32, 128), BF16)]
    + [((RES, 32, 128), BF16), ((RES, 8, 32, 128), BF16)]
    + [((2048, 128), BF16)]
    + [((32, 128, 256), BF16)]
    + [((512, 256), BF16)]
    + [((32, 32, 2048), BF16)]
    + [((512, 1024), BF16)]
    + [((512, 256), F32)]
    + [((4, 16, 32, 128), BF16)] * 2
    + [((RES, 8, 32, 128), BF16)] * 2
    + [((RES, SEQ, 64), BF16)]
    + [((16, 64, 128), BF16)] * 2
    + [((16, 16, 128), BF16)] * 2
    + [((80, 128), BF16), ((8, 80, 128), BF16)]
    + [((80, 128), BF16), ((16, 80, 128), BF16)]
    + [((N_DAP, 8, 128), BF16)] * 2
)
SEMAPHORES = 39


def body(
    aligned_rows,
    asking_projection,
    lookup_projection,
    content_projection,
    sigmoid_projection,
    sigmoid_shift,
    result_projection,
    tensor_mean_projections,
    twofold_projection,
    refreshed_rows_adjoint,
    twofold_change_adjoint,
):
    whole = pl.BlockSpec(memory_space=pltpu.VMEM)
    results = (
        jax.ShapeDtypeStruct((512, CH), BF16),
        jax.ShapeDtypeStruct((1024, 128), F32),
        jax.ShapeDtypeStruct((64, CH), F32),
        jax.ShapeDtypeStruct((128, SEQ), F32),
    )
    found = pl.pallas_call(
        kernel,
        out_shape=results,
        in_specs=[whole] * 11,
        out_specs=(whole,) * 4,
        scratch_shapes=[pltpu.VMEM(shape, kind) for shape, kind in SCRATCH]
        + [pltpu.SemaphoreType.DMA((SEMAPHORES,)), pltpu.SemaphoreType.DMA((SEMAPHORES,))],
        compiler_params=pltpu.CompilerParams(
            collective_id=0, has_side_effects=True, vmem_limit_bytes=56 * 2**20
        ),
        name="evoformer_backward",
    )(
        aligned_rows.reshape(512, CH),
        asking_projection,
        lookup_projection,
        content_projection,
        sigmoid_projection,
        sigmoid_shift.reshape(1, CH),
        result_projection,
        tensor_mean_projections.T,
        twofold_projection,
        refreshed_rows_adjoint.reshape(512, CH),
        twofold_change_adjoint.reshape(2048, 128),
    )
    anywhere = pl.BlockSpec(memory_space=pl.ANY)
    out, pwg, owg, rfg = pl.pallas_call(
        settle,
        out_shape=results,
        in_specs=[anywhere] * 4,
        out_specs=(anywhere,) * 4,
        scratch_shapes=[pltpu.VMEM(result.shape, result.dtype) for result in results]
        + [pltpu.SemaphoreType.DMA((4,)), pltpu.SemaphoreType.DMA((4,))],
        name="settle",
    )(*found)
    return (
        out.reshape(1, 512, CH),
        pwg,
        owg.T,
        rfg.reshape(RES, 32, SEQ).transpose(2, 0, 1),
    )


def solution(mesh):
    split = P(("dp", "dap"), None, None)
    in_specs = (split,) + (P(),) * 8 + (split, split)
    out_specs = (split, P("dp", None), P("dp", None), P("dp", "dap", None))
    return jax.shard_map(body, mesh=mesh, in_specs=in_specs, out_specs=out_specs, check_vma=False)
```

time: 84.4 us -> 69.5 us (0.82)
  Pallas kernels: 76.2 us -> 68.7 us
  local copies, waits for them, and re-layouts: 7.2 us -> 0 us
    pallas_call x1 -> x2, Pallas kernels: 76.2 us -> 68.7 us  [the longest x1 66.7 us: body(): pl.pallas_call(kernel, out_shape=results, in_specs=[whole] * 11, out_spec...]
    unnamed x6 -> x0, local copies, waits for them, and re-layouts: 5.63 us -> none
    pallas_call x1 -> x0, local copies, waits for them, and re-layouts: 1.57 us -> none  [body(): pl.pallas_call(kernel, out_shape=(jax.ShapeDtypeStruct((512, CH), BF16),...]
where the time goes in v2:
time: 69.5 us; the launch traced here: 69.4 us
  Pallas kernels  68.7 us (99%)
    pallas_call x1, Pallas kernels, body(): pl.pallas_call(kernel, out_shape=results, in_specs=[whole] * 11, out_spec...  66.7 us
    pallas_call x1, Pallas kernels, body(): pl.pallas_call(settle, out_shape=results, in_specs=[anywhere] * 4, out_sp...  2.02 us

profile of v2, /device:TPU:1, one launch (start us, length us, event | category | flops | bytes accessed | tf_op | source)
XLA Modules:
  0.0 69.4 jit_solution(7433382721755242745)
XLA Ops:
  0.6 66.7 %evoformer_backward.1 = (bf16[512,256]{1,0:T(8,128)(2,1)}, f32[1024,128]{1,0:T(8,128)}, f32[64,256]{1,0:T(8,128)}, f32[128,128]{1,0:T(8,128)}) custom-call(bf16[512,256]{1,0:T(8,128)(2,1)} %bitcast.11, bf16[256,256]{1,0:T(8,128)(2,1)} %wq_ref.1, bf16[256,256]{1,0:T(8,128)(2,1)} %wk_ref.1, bf16[256,256]{1,0:T(8,128)(2,1)} %wv_ref.1, bf16[256,256]{1,0:T(8,128)(2,1)} %wg_ref.1, ...), custom_call_target="tpu_custom_call" | custom-call | tf_op jit(solution)/shard_map/evoformer_backward/pallas_call | solution.py:470
  67.4 2.0 %settle.1 = (bf16[512,256]{1,0:T(8,128)(2,1)}, f32[1024,128]{1,0:T(8,128)}, f32[64,256]{1,0:T(8,128)}, f32[128,128]{1,0:T(8,128)}) custom-call(bf16[512,256]{1,0:T(8,128)(2,1)} %get-tuple-element.12.refs_0_, f32[1024,128]{1,0:T(8,128)} %get-tuple-element.13.refs_1_, f32[64,256]{1,0:T(8,128)} %get-tuple-element.14.refs_2_, f32[128,128]{1,0:T(8,128)} %get-tuple-element.15.refs_3_), custom_call_target="tpu_custom_call" | custom-call | tf_op jit(solution)/shard_map/settle/pallas_call | solution.py:495

commit v3 on v2

--- a/solution.py
+++ b/solution.py
@@ -98,15 +98,24 @@
 
 
 def kernel(
+    rows_in, wq_in, wk_in, wv_in, wg_in, shift_in, wo_in, wf_in, wp_in, adj_in, pair_in,
+    out_ref, pwg_ref, owg_ref, rfg_ref,
     rows_ref, wq_ref, wk_ref, wv_ref, wg_ref, shift_ref, wo_ref, wf_ref, wp_ref, adj_ref, pair_ref,
-    out_ref, pwg_ref, owg_ref, rfg_ref,
     xs, xr, us, ur, gs, gr, t32, u32, hat_in, sc_in, gate, att, q_all, k_all,
     v_all, w_all, nmid, hat_mid, sc_mid, ls, lg, rs, rg, lp, g2, w2, y, xp, pacc, gls, glr, grs, grr,
-    dcat, ps, pr, qs, qr, zs, zr, fs, fr, os, orr, send, recv,
+    dcat, ps, pr, qs, qr, zs, zr, fs, fr, os, orr, w_t, send, recv, bring,
 ):
     me = lax.axis_index("dap")
     whole_group, wide_group, long_group = groups(me)
     wide, along = wide_group[0], long_group[0]
+    pairs = (
+        (rows_in, rows_ref), (pair_in, pair_ref), (adj_in, adj_ref), (wp_in, wp_ref), (wq_in, wq_ref),
+        (wk_in, wk_ref), (wv_in, wv_ref), (wg_in, wg_ref), (shift_in, shift_ref), (wo_in, wo_ref),
+        (wf_in, wf_ref),
+    )
+    brought = [pltpu.make_async_copy(a, b, bring.at[n]) for n, (a, b) in enumerate(pairs)]
+    for copy in brought:
+        copy.start()
     bar = pltpu.get_barrier_semaphore()
     for device, _ in whole_group[1]:
         pl.semaphore_signal(bar, inc=1, device_id={"dap": device}, device_id_type=MESH)
@@ -120,17 +129,21 @@
     def push_z(src, dst, sem, spread):
         push(long_group, src, dst, send.at[sem], recv.at[sem], spread)
 
-    def stage_rows(ref, dst):
+    def stage_rows(ref):
         u32[pl.ds(0, 512, stride=2), :] = ref[:, 0:128].astype(F32)
         u32[pl.ds(1, 512, stride=2), :] = ref[:, 128:256].astype(F32)
-        dst[...] = u32[...].reshape(N_DAP, 8, 128).astype(BF16)
-
-    stage_rows(rows_ref, xs)
-    xr[me] = xs[me]
+
+    brought[0].wait()
+    stage_rows(rows_ref)
+    for p in range(2):
+        xs[p] = u32[...].reshape(N_DAP, 8, 128)[:, 4 * p:4 * p + 4, :].astype(BF16)
+        xr[p, me] = xs[p, me]
     pl.semaphore_wait(bar, N_DAP - 1)
 
-    push_all(xs, xr, 0)
-
+    for p in range(2):
+        push_all(xs.at[p], xr.at[p], p)
+
+    brought[1].wait()
     t32[...] = pair_ref[...].astype(F32)
 
     def stage_pair(at, carry):
@@ -146,7 +159,10 @@
     gr[wide] = gs[wide]
     push_wide(gs, gr, 8, True)
 
-    stage_rows(adj_ref, us)
+    for copy in brought[2:]:
+        copy.wait()
+    stage_rows(adj_ref)
+    us[...] = u32[...].reshape(N_DAP, 8, 128).astype(BF16)
     ur[me] = us[me]
     g2[...] = jnp.zeros_like(g2)
     for c_hi in range(16):
@@ -155,9 +171,6 @@
                 wp_ref[(2 * c_hi + c_lo) * 32:(2 * c_hi + c_lo + 1) * 32, :].astype(F32) * (1.0 / SEQ)
             ).astype(BF16)
 
-    drain(xr, N_DAP, recv.at[0])
-    u32[...] = xr[...].astype(F32).reshape(1024, 128)
-
     lane_head = lax.broadcasted_iota(jnp.int32, (1, CH), 1) // HEAD_DIM
     masks = [(lane_head == h).astype(F32).astype(BF16) for h in range(HEADS)]
 
@@ -167,9 +180,9 @@
     def side_by_side(value):
         return jnp.concatenate([value[h * 128:(h + 1) * 128, :] for h in range(HEADS)], axis=1)
 
-    def forward(r, carry):
+    def forward(r, n):
         x = jnp.concatenate(
-            [u32[pl.ds(2 * r + half, SEQ, stride=8), :] for half in range(2)], axis=1
+            [u32[pl.ds(2 * n + half, SEQ, stride=4), :] for half in range(2)], axis=1
         )
         hat, scale = standardize(x)
         hat_in[r] = hat
@@ -197,98 +210,87 @@
         normed = hat.astype(BF16)
         nmid[r] = normed
         factors = nt(wf_ref[...], normed).astype(BF16)
-        ls[r] = factors[0:32, :]
-        rs[r] = factors[32:64, :]
-        push_wide(ls.at[r], lg.at[r], 11 + r, False)
-        push_z(rs.at[r], rg.at[r], 15 + r, False)
-        lg[r, wide] = ls[r]
-        rg[r, along] = rs[r]
+        return factors
+
+    def forward_pair(p, carry):
+        drain(xr.at[p], N_DAP, recv.at[p])
+        u32[0:512, :] = xr[p].astype(F32).reshape(512, 128)
+        both = [forward(2 * p + n, n) for n in range(2)]
+        ls[p] = jnp.concatenate([factors[0:32, :] for factors in both], axis=0)
+        rs[p] = jnp.concatenate([factors[32:64, :] for factors in both], axis=0)
+        push_z(rs.at[p], rg.at[p], 15 + p, False)
+        push_wide(ls.at[p], lg.at[p], 11 + p, False)
+        lg[p, wide] = ls[p]
+        rg[p, along] = rs[p]
         return carry
 
-    lax.fori_loop(0, RES, forward, 0)
-
-    push_all(us, ur, 1)
+    lax.fori_loop(0, 2, forward_pair, 0)
+
+    push_all(us, ur, 2)
 
     drain(gr, N_WIDE, recv.at[8])
     t32[...] = gr[...].astype(F32).reshape(2048, 128)
 
-    def build(jn, carry):
+    for jn in range(32):
+        from_j = (jn // 16 * 2 + jn % 2) * 8 + jn % 16 // 2
         part = jnp.concatenate(
-            [t32[pl.ds(r * 32 + jn, 16, stride=128), :] for r in range(RES)], axis=0
+            [t32[pl.ds(r * 32 + from_j, 16, stride=128), :] for r in range(RES)], axis=0
         ).astype(BF16)
         g2[jn, 0:64, 0:128] = part
         g2[jn, 64:128, 128:256] = part
-        return carry
-
-    lax.fori_loop(0, 32, build, 0)
-
-    def pair_grad(at, carry):
-        res = nt(w2[...], g2[pl.ds(at * 4, 4)].reshape(512, 256)).astype(BF16)
+
+    for at in range(8):
+        res = nt(w2[...], g2[at * 4:at * 4 + 4].reshape(512, 256)).astype(BF16)
         for jj in range(4):
             for c_hi in range(16):
                 y[at * 4 + jj, :, c_hi * 128:(c_hi + 1) * 128] = res[
                     c_hi * 32:(c_hi + 1) * 32, jj * 128:(jj + 1) * 128
                 ]
-        return carry
-
-    lax.fori_loop(0, 8, pair_grad, 0)
-
     for r in range(RES):
-        drain(lg.at[r], N_WIDE, recv.at[11 + r])
+        w_t[r] = w_all[r].astype(BF16).T
+
+    for p in range(2):
+        drain(lg.at[p], N_WIDE, recv.at[11 + p])
     t32[...] = lg[...].astype(F32).reshape(2048, 128)
-
-    def order_left(c, carry):
+    for c in range(32):
         part = jnp.concatenate(
-            [t32[pl.ds(r * 512 + c, 16, stride=32), :] for r in range(RES)], axis=0
+            [
+                t32[pl.ds((r // 2) * 1024 + (r % 2) * 32 + c, 16, stride=64), :]
+                for r in range(RES)
+            ],
+            axis=0,
         )
-        lp[pl.ds(pl.multiple_of(c * 64, 64), 64), :] = part.astype(BF16)
-        return carry
-
-    lax.fori_loop(0, 32, order_left, 0)
-
-    for r in range(RES):
-        drain(rg.at[r], N_Z, recv.at[15 + r])
+        lp[c * 64:(c + 1) * 64, :] = part.astype(BF16)
+
+    for p in range(2):
+        res = nn(y[p * 16:(p + 1) * 16].reshape(512, 2048), lp[...]).astype(BF16)
+        grs[p] = res.reshape(8, 64, 128)
+    for p in range(2):
+        grr[p, along] = grs[p, along]
+        push_z(grs.at[p], grr.at[p], 19 + p, True)
+
+    for p in range(2):
+        drain(rg.at[p], N_Z, recv.at[15 + p])
     rg_t = rg[...].reshape(1024, 128).astype(F32).T.astype(BF16)
-
-    def left_grad(at, carry):
-        col = pl.multiple_of(at * 512, 512)
-        res = nn(rg_t, y[:, :, pl.ds(col, 512)].reshape(1024, 512))
-        t32[0:512, :] = res.T
-        for m in range(16):
-            gls[at, m] = jnp.concatenate(
-                [t32[pl.ds(m + 16 * r, 8, stride=64), :] for r in range(RES)], axis=0
-            ).astype(BF16)
-        glr[at, wide] = gls[at, wide]
-        push_wide(gls.at[at], glr.at[at], 23 + at, True)
-        return carry
-
-    lax.fori_loop(0, 4, left_grad, 0)
-
-    def right_grad(r, carry):
-        res = nn(y[pl.ds(r * 8, 8)].reshape(256, 2048), lp[...]).astype(BF16)
-        grs[r] = res.reshape(8, 32, 128)
-        grr[r, along] = grs[r, along]
-        push_z(grs.at[r], grr.at[r], 19 + r, True)
-        return carry
-
-    lax.fori_loop(0, RES, right_grad, 0)
-
-    pacc[...] = jnp.zeros_like(pacc)
-
-    def pair_weight(r, carry):
-        rows = rg[r].reshape(256, 128)
-        for group in range(4):
-            res = nt(rows, lp[group * 512:(group + 1) * 512, :]).astype(BF16)
-            for jj in range(8):
-                for cc in range(4):
-                    c_hi = group * 4 + cc
-                    xp[c_hi * 32:(c_hi + 1) * 32, jj * 128:(jj + 1) * 128] = res[
-                        jj * 32:(jj + 1) * 32, cc * 128:(cc + 1) * 128
-                    ]
-        pacc[...] += nn(xp[...], g2[pl.ds(r * 8, 8)].reshape(1024, 256))
-        return carry
-
-    lax.fori_loop(0, RES, pair_weight, 0)
+    for at in range(4):
+        res = nn(rg_t, y[:, :, at * 512:(at + 1) * 512].reshape(1024, 512))
+        t32[at * 512:(at + 1) * 512, :] = res.T
+    for m in range(16):
+        gls[m] = jnp.concatenate(
+            [t32[pl.ds(m + 16 * r, 32, stride=64), :] for r in range(RES)], axis=0
+        ).astype(BF16)
+    glr[wide] = gls[wide]
+    push_wide(gls, glr, 23, True)
+
+    for group in range(4):
+        res = nt(rg[...].reshape(1024, 128), lp[group * 512:(group + 1) * 512, :]).astype(BF16)
+        for jn in range(32):
+            for cc in range(4):
+                c_hi = group * 4 + cc
+                xp[c_hi * 32:(c_hi + 1) * 32, jn * 128:(jn + 1) * 128] = res[
+                    jn * 32:(jn + 1) * 32, cc * 128:(cc + 1) * 128
+                ]
+    pacc[...] = nn(xp[...], g2[...].reshape(4096, 256))
 
     for m in range(16):
         part = pacc[m * 32:(m + 1) * 32, :] * (1.0 / SEQ)
@@ -296,16 +298,15 @@
     pr[wide] = ps[wide]
     push_wide(ps, pr, 27, True)
 
-    for r in range(RES):
-        drain(grr.at[r], N_Z, recv.at[19 + r])
-    right_sum = jnp.sum(grr[...].astype(F32), axis=1)
-    for at in range(4):
-        drain(glr.at[at], N_WIDE, recv.at[23 + at])
-    left_sum = jnp.sum(glr[...].astype(F32), axis=1)
+    for p in range(2):
+        drain(grr.at[p], N_Z, recv.at[19 + p])
+    right_sum = jnp.sum(grr[...].astype(F32), axis=1).reshape(128, SEQ)
+    drain(glr, N_WIDE, recv.at[23])
+    left_sum = jnp.sum(glr[...].astype(F32), axis=0)
     owg = jnp.zeros((64, CH), F32)
     for r in range(RES):
         both = jnp.concatenate(
-            [left_sum[at, r * 8:(r + 1) * 8, :] for at in range(4)] + [right_sum[r]], axis=0
+            [left_sum[r * 32:(r + 1) * 32, :], right_sum[r * 32:(r + 1) * 32, :]], axis=0
         )
         owg = owg + nn(both.astype(BF16), nmid[r])
         dcat[r] = both.T.astype(BF16)
@@ -322,10 +323,10 @@
     qr[wide] = qs[wide]
     push_wide(qs, qr, 38, True)
 
-    drain(ur, N_DAP, recv.at[1])
+    drain(ur, N_DAP, recv.at[2])
     t32[1024:2048, :] = ur[...].astype(F32).reshape(1024, 128)
 
-    def backward(r, carry):
+    def backward(r, n):
         grad = nn(dcat[r], wf_ref[...]).astype(BF16).astype(F32)
         dmid = standardize_back(grad, hat_mid[r], sc_mid[r][:, 0:1]).astype(BF16).astype(F32)
         arriving = jnp.concatenate(
@@ -343,17 +344,23 @@
         dq = nn(side_by_side(ds.astype(BF16)), blocks(k_all[r])).astype(BF16)
         dq = (dq.astype(F32) * HEAD_DIM ** (-0.5)).astype(BF16)
         dk = nn(ds.T.astype(BF16), blocks(q_all[r])).astype(BF16)
-        dv = nn(w.T.astype(BF16), datt).astype(BF16)
+        dv = nn(w_t[r], datt).astype(BF16)
         dnorm = (
             nt(dq, wq_ref[...]) + nt(dk, wk_ref[...]) + nt(dv, wv_ref[...]) + nt(dpre, wg_ref[...])
         ).astype(BF16).astype(F32)
         dx = standardize_back(dnorm, hat_in[r], sc_in[r][:, 0:1]).astype(BF16).astype(F32)
         total = gm + dx
         for half in range(2):
-            u32[pl.ds(2 * r + half, SEQ, stride=8), :] = total[:, half * 128:(half + 1) * 128]
-        return carry
-
-    lax.fori_loop(0, 2, backward, 0)
+            u32[pl.ds(2 * n + half, SEQ, stride=4), :] = total[:, half * 128:(half + 1) * 128]
+
+    def backward_pair(p):
+        for n in range(2):
+            backward(2 * p + n, n)
+        os[p] = u32[0:512, :].reshape(N_DAP, 4, 128).astype(BF16)
+        orr[p, me] = os[p, me]
+        push_all(os.at[p], orr.at[p], 3 + p)
+
+    backward_pair(0)
 
     drain(pr, N_WIDE, recv.at[27])
     drain(qr, N_WIDE, recv.at[38])
@@ -362,24 +369,22 @@
     zr[along] = zs[...]
     push_z(zs, zr, 28, False)
 
-    lax.fori_loop(2, RES, backward, 0)
-
-    os[...] = u32[...].reshape(N_DAP, 8, 128).astype(BF16)
-    orr[me] = os[me]
-    push_all(os, orr, 2)
+    backward_pair(1)
+
     drain(zr, N_Z, recv.at[28])
     fs[...] = jnp.sum(zr[...].astype(F32), axis=0).astype(BF16)
     fr[wide] = fs[...]
     push_wide(fs, fr, 29, False)
 
-    rfg_ref[...] = right_sum.reshape(128, SEQ)
-    drain(xr, N_DAP, send.at[0])
-    drain(ur, N_DAP, send.at[1])
-    for r in range(RES):
-        drain(lg.at[r], N_WIDE, send.at[11 + r])
-        drain(rg.at[r], N_Z, send.at[15 + r])
-        drain(grr.at[r], N_Z, send.at[19 + r])
-        drain(glr.at[r], N_WIDE, send.at[23 + r])
+    rfg_ref[...] = right_sum
+    drain(xr.at[0], N_DAP, send.at[0])
+    drain(xr.at[1], N_DAP, send.at[1])
+    drain(ur, N_DAP, send.at[2])
+    for p in range(2):
+        drain(lg.at[p], N_WIDE, send.at[11 + p])
+        drain(rg.at[p], N_Z, send.at[15 + p])
+        drain(grr.at[p], N_Z, send.at[19 + p])
+    drain(glr, N_WIDE, send.at[23])
     drain(gr, N_WIDE, send.at[8])
     drain(pr, N_WIDE, send.at[27])
     drain(qr, N_WIDE, send.at[38])
@@ -395,28 +400,33 @@
     )
     drain(fr, N_WIDE, send.at[29])
 
-    drain(orr, N_DAP, recv.at[2])
-    u32[...] = orr[...].astype(F32).reshape(1024, 128)
+    for p in range(2):
+        drain(orr.at[p], N_DAP, recv.at[3 + p])
+        t32[0:512, :] = orr[p].astype(F32).reshape(512, 128)
+        for k in range(4):
+            u32[pl.ds(4 * p + k, N_DAP, stride=8), :] = t32[pl.ds(k, N_DAP, stride=4), :]
     out_ref[:, 0:128] = u32[pl.ds(0, 512, stride=2), :].astype(BF16)
     out_ref[:, 128:256] = u32[pl.ds(1, 512, stride=2), :].astype(BF16)
-    drain(orr, N_DAP, send.at[2])
+    drain(orr.at[0], N_DAP, send.at[3])
+    drain(orr.at[1], N_DAP, send.at[4])
 
 
 def settle(*refs):
-    found, results, held, arrive, leave = refs[0:4], refs[4:8], refs[8:12], refs[12], refs[13]
-    ins = [pltpu.make_async_copy(found[n], held[n], arrive.at[n]) for n in range(4)]
-    outs = [pltpu.make_async_copy(held[n], results[n], leave.at[n]) for n in range(4)]
-    for copy in ins:
+    found, results, sems = refs[0:4], refs[4:8], refs[8]
+    copies = [pltpu.make_async_copy(found[n], results[n], sems.at[n]) for n in range(4)]
+    for copy in copies:
         copy.start()
-    for n in range(4):
-        ins[n].wait()
-        outs[n].start()
-    for copy in outs:
+    for copy in copies:
         copy.wait()
 
 
 SCRATCH = (
-    [((N_DAP, 8, 128), BF16)] * 4
+    [((512, CH), BF16)]
+    + [((CH, CH), BF16)] * 4
+    + [((1, CH), F32), ((CH, CH), BF16), ((64, CH), BF16), ((1024, 128), BF16)]
+    + [((512, CH), BF16), ((2048, 128), BF16)]
+    + [((2, N_DAP, 4, 128), BF16)] * 2
+    + [((N_DAP, 8, 128), BF16)] * 2
     + [((16, 128, 128), BF16)] * 2
     + [((2048, 128), F32), ((1024, 128), F32)]
     + [((RES, SEQ, CH), F32)]
@@ -427,22 +437,23 @@
     + [((RES, SEQ, CH), BF16)]
     + [((RES, SEQ, CH), F32)]
     + [((RES, SEQ, 128), F32)]
-    + [((RES, 32, 128), BF16), ((RES, 16, 32, 128), BF16)]
-    + [((RES, 32, 128), BF16), ((RES, 8, 32, 128), BF16)]
+    + [((2, 64, 128), BF16), ((2, 16, 64, 128), BF16)]
+    + [((2, 64, 128), BF16), ((2, 8, 64, 128), BF16)]
     + [((2048, 128), BF16)]
     + [((32, 128, 256), BF16)]
     + [((512, 256), BF16)]
     + [((32, 32, 2048), BF16)]
-    + [((512, 1024), BF16)]
+    + [((512, 4096), BF16)]
     + [((512, 256), F32)]
-    + [((4, 16, 32, 128), BF16)] * 2
-    + [((RES, 8, 32, 128), BF16)] * 2
+    + [((16, 128, 128), BF16)] * 2
+    + [((2, 8, 64, 128), BF16)] * 2
     + [((RES, SEQ, 64), BF16)]
     + [((16, 64, 128), BF16)] * 2
     + [((16, 16, 128), BF16)] * 2
     + [((80, 128), BF16), ((8, 80, 128), BF16)]
     + [((80, 128), BF16), ((16, 80, 128), BF16)]
-    + [((N_DAP, 8, 128), BF16)] * 2
+    + [((2, N_DAP, 4, 128), BF16)] * 2
+    + [((RES, SEQ, HEADS * SEQ), BF16)]
 )
 SEMAPHORES = 39
 
@@ -461,6 +472,7 @@
     twofold_change_adjoint,
 ):
     whole = pl.BlockSpec(memory_space=pltpu.VMEM)
+    anywhere = pl.BlockSpec(memory_space=pl.ANY)
     results = (
         jax.ShapeDtypeStruct((512, CH), BF16),
         jax.ShapeDtypeStruct((1024, 128), F32),
@@ -469,11 +481,12 @@
     )
     found = pl.pallas_call(
         kernel,
-        out_shape=results,
-        in_specs=[whole] * 11,
+        out_shape=tuple(pltpu.VMEM(result.shape, result.dtype) for result in results),
+        in_specs=[anywhere] * 11,
         out_specs=(whole,) * 4,
         scratch_shapes=[pltpu.VMEM(shape, kind) for shape, kind in SCRATCH]
-        + [pltpu.SemaphoreType.DMA((SEMAPHORES,)), pltpu.SemaphoreType.DMA((SEMAPHORES,))],
+        + [pltpu.SemaphoreType.DMA((SEMAPHORES,)), pltpu.SemaphoreType.DMA((SEMAPHORES,))]
+        + [pltpu.SemaphoreType.DMA((11,))],
         compiler_params=pltpu.CompilerParams(
             collective_id=0, has_side_effects=True, vmem_limit_bytes=56 * 2**20
         ),
@@ -491,16 +504,14 @@
         refreshed_rows_adjoint.reshape(512, CH),
         twofold_change_adjoint.reshape(2048, 128),
     )
-    anywhere = pl.BlockSpec(memory_space=pl.ANY)
     out, pwg, owg, rfg = pl.pallas_call(
         settle,
         out_shape=results,
         in_specs=[anywhere] * 4,
         out_specs=(anywhere,) * 4,
-        scratch_shapes=[pltpu.VMEM(result.shape, result.dtype) for result in results]
-        + [pltpu.SemaphoreType.DMA((4,)), pltpu.SemaphoreType.DMA((4,))],
+        scratch_shapes=[pltpu.SemaphoreType.DMA((4,))],
         name="settle",
-    )(*found)
+    )(*[pltpu.with_memory_space_constraint(array, pltpu.VMEM) for array in found])
     return (
         out.reshape(1, 512, CH),
         pwg,

time: 69.5 us -> 63.5 us (0.914)
  Pallas kernels: 68.7 us -> 62.6 us
    pallas_call x1, Pallas kernels: 66.7 us -> 61.6 us  [body(): pl.pallas_call(kernel, out_shape=tuple((pltpu.VMEM(result.shape, result.d...]
    pallas_call x1, Pallas kernels: 2.02 us -> 0.95 us  [body(): pl.pallas_call(settle, out_shape=results, in_specs=[anywhere] * 4, out_sp...]
where the time goes in v3:
time: 63.5 us; the launch traced here: 63.4 us
  Pallas kernels  62.6 us (99%)
  between operations  0.8 us (1%)
    pallas_call x1, Pallas kernels, body(): pl.pallas_call(kernel, out_shape=tuple((pltpu.VMEM(result.shape, result.d...  61.6 us

profile of v3, /device:TPU:1, one launch (start us, length us, event | category | flops | bytes accessed | tf_op | source)
XLA Modules:
  0.0 63.4 jit_solution(18259142486763479026)
XLA Ops:
  0.6 61.6 %evoformer_backward.1 = (bf16[512,256]{1,0:T(8,128)(2,1)S(1)}, f32[1024,128]{1,0:T(8,128)S(1)}, f32[64,256]{1,0:T(8,128)S(1)}, f32[128,128]{1,0:T(8,128)S(1)}) custom-call(bf16[512,256]{1,0:T(8,128)(2,1)} %bitcast.11, bf16[256,256]{1,0:T(8,128)(2,1)} %wq_in.1, bf16[256,256]{1,0:T(8,128)(2,1)} %wk_in.1, bf16[256,256]{1,0:T(8,128)(2,1)} %wv_in.1, ...), custom_call_target="tpu_custom_call" | custom-call | tf_op jit(solution)/shard_map/evoformer_backward/pallas_call | solution.py:482
  62.3 0.9 %settle.1 = (bf16[512,256]{1,0:T(8,128)(2,1)}, f32[1024,128]{1,0:T(8,128)}, f32[64,256]{1,0:T(8,128)}, f32[128,128]{1,0:T(8,128)}) custom-call(bf16[512,256]{1,0:T(8,128)(2,1)S(1)} %get-tuple-element.12.refs_0_, f32[1024,128]{1,0:T(8,128)S(1)} %get-tuple-element.13.refs_1_, f32[64,256]{1,0:T(8,128)S(1)} %get-tuple-element.14.refs_2_, ...), custom_call_target="tpu_custom_call" | custom-call | tf_op jit(solution)/shard_map/settle/pallas_call | solution.py:507

commit v4 on v3

--- a/solution.py
+++ b/solution.py
@@ -60,7 +60,18 @@
         line = xs[dx] + ys[dy]
         wide.append((line + z * 2 + cores[dc], lax.div(line, 8) + cores[dc]))
     long = [(xs[0] + ys[0] + twice[dz] + core, zs[dz]) for dz in (4, 3, 5, 2, 6, 1, 7)]
-    return (me, everyone), (lax.div(xs[0] + ys[0], 8) + core, wide), (z, long)
+    level = []
+    for dx, dy in ((1, 2), (0, 2), (1, 1), (1, 3), (0, 1), (0, 3), (1, 0)):
+        line = xs[dx] + ys[dy]
+        level.append((line + z * 2 + core, lax.div(line, 16)))
+    line = xs[0] + ys[0]
+    return (
+        (me, everyone),
+        (lax.div(line, 8) + core, wide),
+        (z, long),
+        (lax.div(line, 16), level),
+        line + z * 2 + 1 - core,
+    )
 
 
 def push(group, src, dst, send_sem, recv_sem, spread):
@@ -102,12 +113,13 @@
     out_ref, pwg_ref, owg_ref, rfg_ref,
     rows_ref, wq_ref, wk_ref, wv_ref, wg_ref, shift_ref, wo_ref, wf_ref, wp_ref, adj_ref, pair_ref,
     xs, xr, us, ur, gs, gr, t32, u32, hat_in, sc_in, gate, att, q_all, k_all,
-    v_all, w_all, nmid, hat_mid, sc_mid, ls, lg, rs, rg, lp, g2, w2, y, xp, pacc, gls, glr, grs, grr,
-    dcat, ps, pr, qs, qr, zs, zr, fs, fr, os, orr, w_t, send, recv, bring,
+    v_all, w_all, nmid, hat_mid, sc_mid, ls, lg, rs, rg, lp, g2, w2, y, xp, pacc, gls, glx, glo, glr, grs, grr,
+    dcat, ps, pr, qs, qr, zs, zr, zq, zqr, fs, fr, fq, fqr, os, orr, w_t, send, recv, bring,
 ):
     me = lax.axis_index("dap")
-    whole_group, wide_group, long_group = groups(me)
-    wide, along = wide_group[0], long_group[0]
+    whole_group, wide_group, long_group, level_group, sibling = groups(me)
+    wide, along, level = wide_group[0], long_group[0], level_group[0]
+    core_here = lax.rem(me, 2)
     pairs = (
         (rows_in, rows_ref), (pair_in, pair_ref), (adj_in, adj_ref), (wp_in, wp_ref), (wq_in, wq_ref),
         (wk_in, wk_ref), (wv_in, wv_ref), (wg_in, wg_ref), (shift_in, shift_ref), (wo_in, wo_ref),
@@ -276,13 +288,24 @@
         res = nn(rg_t, y[:, :, at * 512:(at + 1) * 512].reshape(1024, 512))
         t32[at * 512:(at + 1) * 512, :] = res.T
     for m in range(16):
-        gls[m] = jnp.concatenate(
+        gls[m % 2, m // 2] = jnp.concatenate(
             [t32[pl.ds(m + 16 * r, 32, stride=64), :] for r in range(RES)], axis=0
         ).astype(BF16)
-    glr[wide] = gls[wide]
-    push_wide(gls, glr, 23, True)
+    pltpu.make_async_remote_copy(
+        src_ref=gls.at[1 - core_here],
+        dst_ref=glx,
+        send_sem=send.at[24],
+        recv_sem=recv.at[24],
+        device_id={"dap": sibling},
+        device_id_type=MESH,
+    ).start()
 
     for group in range(4):
+        if group == 2:
+            pltpu.make_async_copy(glx, glx, recv.at[24]).wait()
+            glo[...] = (gls[core_here].astype(F32) + glx[...].astype(F32)).astype(BF16)
+            glr[level] = glo[level]
+            push(level_group, glo, glr, send.at[23], recv.at[23], True)
         res = nt(rg[...].reshape(1024, 128), lp[group * 512:(group + 1) * 512, :]).astype(BF16)
         for jn in range(32):
             for cc in range(4):
@@ -301,7 +324,7 @@
     for p in range(2):
         drain(grr.at[p], N_Z, recv.at[19 + p])
     right_sum = jnp.sum(grr[...].astype(F32), axis=1).reshape(128, SEQ)
-    drain(glr, N_WIDE, recv.at[23])
+    drain(glr, N_Z, recv.at[23])
     left_sum = jnp.sum(glr[...].astype(F32), axis=0)
     owg = jnp.zeros((64, CH), F32)
     for r in range(RES):
@@ -353,28 +376,36 @@
         for half in range(2):
             u32[pl.ds(2 * n + half, SEQ, stride=4), :] = total[:, half * 128:(half + 1) * 128]
 
-    def backward_pair(p):
-        for n in range(2):
-            backward(2 * p + n, n)
+    def send_pair(p):
         os[p] = u32[0:512, :].reshape(N_DAP, 4, 128).astype(BF16)
         orr[p, me] = os[p, me]
         push_all(os.at[p], orr.at[p], 3 + p)
 
-    backward_pair(0)
+    for n in range(2):
+        backward(n, n)
 
     drain(pr, N_WIDE, recv.at[27])
-    drain(qr, N_WIDE, recv.at[38])
-    zs[0:64, :] = jnp.sum(pr[...].astype(F32), axis=0).astype(BF16)
-    zs[64:80, :] = jnp.sum(qr[...].astype(F32), axis=0).astype(BF16)
+    zs[...] = jnp.sum(pr[...].astype(F32), axis=0).astype(BF16)
     zr[along] = zs[...]
     push_z(zs, zr, 28, False)
-
-    backward_pair(1)
+    send_pair(0)
+
+    for n in range(2):
+        backward(2 + n, n)
+    drain(qr, N_WIDE, recv.at[38])
+    zq[...] = jnp.sum(qr[...].astype(F32), axis=0).astype(BF16)
+    zqr[along] = zq[...]
+    push_z(zq, zqr, 39, False)
+    send_pair(1)
 
     drain(zr, N_Z, recv.at[28])
     fs[...] = jnp.sum(zr[...].astype(F32), axis=0).astype(BF16)
     fr[wide] = fs[...]
     push_wide(fs, fr, 29, False)
+    drain(zqr, N_Z, recv.at[39])
+    fq[...] = jnp.sum(zqr[...].astype(F32), axis=0).astype(BF16)
+    fqr[wide] = fq[...]
+    push_wide(fq, fqr, 40, False)
 
     rfg_ref[...] = right_sum
     drain(xr.at[0], N_DAP, send.at[0])
@@ -384,21 +415,25 @@
         drain(lg.at[p], N_WIDE, send.at[11 + p])
         drain(rg.at[p], N_Z, send.at[15 + p])
         drain(grr.at[p], N_Z, send.at[19 + p])
-    drain(glr, N_WIDE, send.at[23])
+    drain(glr, N_Z, send.at[23])
+    pltpu.make_async_copy(glx, glx, send.at[24]).wait()
     drain(gr, N_WIDE, send.at[8])
     drain(pr, N_WIDE, send.at[27])
     drain(qr, N_WIDE, send.at[38])
     drain(zr, N_Z, send.at[28])
+    drain(zqr, N_Z, send.at[39])
 
     drain(fr, N_WIDE, recv.at[29])
+    drain(fqr, N_WIDE, recv.at[40])
     halves = []
     for m in range(16):
-        pwg_ref[m * 64:(m + 1) * 64, :] = fr[m, 0:64, :].astype(F32)
-        halves.append(fr[m, 64:80, :].astype(F32)[0:8, :])
+        pwg_ref[m * 64:(m + 1) * 64, :] = fr[m].astype(F32)
+        halves.append(fqr[m].astype(F32)[0:8, :])
     owg_ref[...] = jnp.concatenate(
         [jnp.concatenate(halves[0:8], axis=0), jnp.concatenate(halves[8:16], axis=0)], axis=1
     )
     drain(fr, N_WIDE, send.at[29])
+    drain(fqr, N_WIDE, send.at[40])
 
     for p in range(2):
         drain(orr.at[p], N_DAP, recv.at[3 + p])
@@ -445,17 +480,20 @@
     + [((32, 32, 2048), BF16)]
     + [((512, 4096), BF16)]
     + [((512, 256), F32)]
-    + [((16, 128, 128), BF16)] * 2
+    + [((2, 8, 128, 128), BF16)]
+    + [((8, 128, 128), BF16)] * 3
     + [((2, 8, 64, 128), BF16)] * 2
     + [((RES, SEQ, 64), BF16)]
     + [((16, 64, 128), BF16)] * 2
     + [((16, 16, 128), BF16)] * 2
-    + [((80, 128), BF16), ((8, 80, 128), BF16)]
-    + [((80, 128), BF16), ((16, 80, 128), BF16)]
+    + [((64, 128), BF16), ((8, 64, 128), BF16)]
+    + [((16, 128), BF16), ((8, 16, 128), BF16)]
+    + [((64, 128), BF16), ((16, 64, 128), BF16)]
+    + [((16, 128), BF16), ((16, 16, 128), BF16)]
     + [((2, N_DAP, 4, 128), BF16)] * 2
     + [((RES, SEQ, HEADS * SEQ), BF16)]
 )
-SEMAPHORES = 39
+SEMAPHORES = 41
 
 
 def body(

time: 63.5 us -> 61.5 us (0.969)
  Pallas kernels: 62.6 us -> 60.6 us
    pallas_call x1, Pallas kernels: 61.6 us -> 59.6 us  [body(): pl.pallas_call(kernel, out_shape=tuple((pltpu.VMEM(result.shape, result.d...]
where the time goes in v4:
time: 61.5 us; the launch traced here: 61.4 us
  Pallas kernels  60.6 us (99%)
  between operations  0.8 us (1%)
    pallas_call x1, Pallas kernels, body(): pl.pallas_call(kernel, out_shape=tuple((pltpu.VMEM(result.shape, result.d...  59.6 us

profile of v4, /device:TPU:1, one launch (start us, length us, event | category | flops | bytes accessed | tf_op | source)
XLA Modules:
  0.0 61.4 jit_solution(5827765473409684579)
XLA Ops:
  0.6 59.6 %evoformer_backward.1 = (bf16[512,256]{1,0:T(8,128)(2,1)S(1)}, f32[1024,128]{1,0:T(8,128)S(1)}, f32[64,256]{1,0:T(8,128)S(1)}, f32[128,128]{1,0:T(8,128)S(1)}) custom-call(bf16[512,256]{1,0:T(8,128)(2,1)} %bitcast.11, bf16[256,256]{1,0:T(8,128)(2,1)} %wq_in.1, bf16[256,256]{1,0:T(8,128)(2,1)} %wk_in.1, bf16[256,256]{1,0:T(8,128)(2,1)} %wv_in.1, ...), custom_call_target="tpu_custom_call" | custom-call | tf_op jit(solution)/shard_map/evoformer_backward/pallas_call | solution.py:520
  60.3 0.9 %settle.1 = (bf16[512,256]{1,0:T(8,128)(2,1)}, f32[1024,128]{1,0:T(8,128)}, f32[64,256]{1,0:T(8,128)}, f32[128,128]{1,0:T(8,128)}) custom-call(bf16[512,256]{1,0:T(8,128)(2,1)S(1)} %get-tuple-element.12.refs_0_, f32[1024,128]{1,0:T(8,128)S(1)} %get-tuple-element.13.refs_1_, f32[64,256]{1,0:T(8,128)S(1)} %get-tuple-element.14.refs_2_, ...), custom_call_target="tpu_custom_call" | custom-call | tf_op jit(solution)/shard_map/settle/pallas_call | solution.py:545

commit v5 on v4

--- a/solution.py
+++ b/solution.py
@@ -74,7 +74,7 @@
     )
 
 
-def push(group, src, dst, send_sem, recv_sem, spread):
+def push(group, sample, src, dst, send_sem, recv_sem, spread):
     mine, others = group
     for device, place in others:
         pltpu.make_async_remote_copy(
@@ -82,7 +82,7 @@
             dst_ref=dst.at[mine],
             send_sem=send_sem,
             recv_sem=recv_sem,
-            device_id={"dap": device},
+            device_id=(device, sample),
             device_id_type=MESH,
         ).start()
 
@@ -117,6 +117,7 @@
     dcat, ps, pr, qs, qr, zs, zr, zq, zqr, fs, fr, fq, fqr, os, orr, w_t, send, recv, bring,
 ):
     me = lax.axis_index("dap")
+    sample = lax.axis_index("dp")
     whole_group, wide_group, long_group, level_group, sibling = groups(me)
     wide, along, level = wide_group[0], long_group[0], level_group[0]
     core_here = lax.rem(me, 2)
@@ -130,16 +131,16 @@
         copy.start()
     bar = pltpu.get_barrier_semaphore()
     for device, _ in whole_group[1]:
-        pl.semaphore_signal(bar, inc=1, device_id={"dap": device}, device_id_type=MESH)
+        pl.semaphore_signal(bar, inc=1, device_id=(device, sample), device_id_type=MESH)
 
     def push_all(src, dst, sem):
-        push(whole_group, src, dst, send.at[sem], recv.at[sem], True)
+        push(whole_group, sample, src, dst, send.at[sem], recv.at[sem], True)
 
     def push_wide(src, dst, sem, spread):
-        push(wide_group, src, dst, send.at[sem], recv.at[sem], spread)
+        push(wide_group, sample, src, dst, send.at[sem], recv.at[sem], spread)
 
     def push_z(src, dst, sem, spread):
-        push(long_group, src, dst, send.at[sem], recv.at[sem], spread)
+        push(long_group, sample, src, dst, send.at[sem], recv.at[sem], spread)
 
     def stage_rows(ref):
         u32[pl.ds(0, 512, stride=2), :] = ref[:, 0:128].astype(F32)
@@ -296,7 +297,7 @@
         dst_ref=glx,
         send_sem=send.at[24],
         recv_sem=recv.at[24],
-        device_id={"dap": sibling},
+        device_id=(sibling, sample),
         device_id_type=MESH,
     ).start()
 
@@ -305,7 +306,7 @@
             pltpu.make_async_copy(glx, glx, recv.at[24]).wait()
             glo[...] = (gls[core_here].astype(F32) + glx[...].astype(F32)).astype(BF16)
             glr[level] = glo[level]
-            push(level_group, glo, glr, send.at[23], recv.at[23], True)
+            push(level_group, sample, glo, glr, send.at[23], recv.at[23], True)
         res = nt(rg[...].reshape(1024, 128), lp[group * 512:(group + 1) * 512, :]).astype(BF16)
         for jn in range(32):
             for cc in range(4):
@@ -374,12 +375,13 @@
         dx = standardize_back(dnorm, hat_in[r], sc_in[r][:, 0:1]).astype(BF16).astype(F32)
         total = gm + dx
         for half in range(2):
-            u32[pl.ds(2 * n + half, SEQ, stride=4), :] = total[:, half * 128:(half + 1) * 128]
+            u32[pl.ds(2 * r + half, SEQ, stride=8), :] = total[:, half * 128:(half + 1) * 128]
 
     def send_pair(p):
-        os[p] = u32[0:512, :].reshape(N_DAP, 4, 128).astype(BF16)
-        orr[p, me] = os[p, me]
-        push_all(os.at[p], orr.at[p], 3 + p)
+        if p == 1:
+            os[...] = u32[...].reshape(N_DAP, 8, 128).astype(BF16)
+            orr[me] = os[me]
+            push_all(os, orr, 3)
 
     for n in range(2):
         backward(n, n)
@@ -435,15 +437,11 @@
     drain(fr, N_WIDE, send.at[29])
     drain(fqr, N_WIDE, send.at[40])
 
-    for p in range(2):
-        drain(orr.at[p], N_DAP, recv.at[3 + p])
-        t32[0:512, :] = orr[p].astype(F32).reshape(512, 128)
-        for k in range(4):
-            u32[pl.ds(4 * p + k, N_DAP, stride=8), :] = t32[pl.ds(k, N_DAP, stride=4), :]
+    drain(orr, N_DAP, recv.at[3])
+    u32[...] = orr[...].astype(F32).reshape(1024, 128)
     out_ref[:, 0:128] = u32[pl.ds(0, 512, stride=2), :].astype(BF16)
     out_ref[:, 128:256] = u32[pl.ds(1, 512, stride=2), :].astype(BF16)
-    drain(orr.at[0], N_DAP, send.at[3])
-    drain(orr.at[1], N_DAP, send.at[4])
+    drain(orr, N_DAP, send.at[3])
 
 
 def settle(*refs):
@@ -490,7 +488,7 @@
     + [((16, 128), BF16), ((8, 16, 128), BF16)]
     + [((64, 128), BF16), ((16, 64, 128), BF16)]
     + [((16, 128), BF16), ((16, 16, 128), BF16)]
-    + [((2, N_DAP, 4, 128), BF16)] * 2
+    + [((N_DAP, 8, 128), BF16)] * 2
     + [((RES, SEQ, HEADS * SEQ), BF16)]
 )
 SEMAPHORES = 41

time: 61.5 us -> 59.9 us (0.974)
  Pallas kernels: 60.6 us -> 59.1 us
    pallas_call x1, Pallas kernels: 59.6 us -> 58.1 us  [body(): pl.pallas_call(kernel, out_shape=tuple((pltpu.VMEM(result.shape, result.d...]
where the time goes in v5:
time: 59.9 us
  Pallas kernels  59.1 us (99%)
  between operations  0.8 us (1%)
    pallas_call x1, Pallas kernels, body(): pl.pallas_call(kernel, out_shape=tuple((pltpu.VMEM(result.shape, result.d...  58.1 us

profile of v5, /device:TPU:1, one launch (start us, length us, event | category | flops | bytes accessed | tf_op | source)
XLA Modules:
  0.0 59.9 jit_solution(6808273801422573981)
XLA Ops:
  0.6 58.1 %evoformer_backward.1 = (bf16[512,256]{1,0:T(8,128)(2,1)S(1)}, f32[1024,128]{1,0:T(8,128)S(1)}, f32[64,256]{1,0:T(8,128)S(1)}, f32[128,128]{1,0:T(8,128)S(1)}) custom-call(bf16[512,256]{1,0:T(8,128)(2,1)} %bitcast.11, bf16[256,256]{1,0:T(8,128)(2,1)} %wq_in.1, bf16[256,256]{1,0:T(8,128)(2,1)} %wk_in.1, bf16[256,256]{1,0:T(8,128)(2,1)} %wv_in.1, ...), custom_call_target="tpu_custom_call" | custom-call | tf_op jit(solution)/shard_map/evoformer_backward/pallas_call | solution.py:518
  58.7 0.9 %settle.1 = (bf16[512,256]{1,0:T(8,128)(2,1)}, f32[1024,128]{1,0:T(8,128)}, f32[64,256]{1,0:T(8,128)}, f32[128,128]{1,0:T(8,128)}) custom-call(bf16[512,256]{1,0:T(8,128)(2,1)S(1)} %get-tuple-element.12.refs_0_, f32[1024,128]{1,0:T(8,128)S(1)} %get-tuple-element.13.refs_1_, f32[64,256]{1,0:T(8,128)S(1)} %get-tuple-element.14.refs_2_, ...), custom_call_target="tpu_custom_call" | custom-call | tf_op jit(solution)/shard_map/settle/pallas_call | solution.py:543

commit v6 on v5

--- a/solution.py
+++ b/solution.py
@@ -127,11 +127,13 @@
         (wf_in, wf_ref),
     )
     brought = [pltpu.make_async_copy(a, b, bring.at[n]) for n, (a, b) in enumerate(pairs)]
-    for copy in brought:
-        copy.start()
+    brought[0].start()
     bar = pltpu.get_barrier_semaphore()
     for device, _ in whole_group[1]:
         pl.semaphore_signal(bar, inc=1, device_id=(device, sample), device_id_type=MESH)
+
+    for copy in brought[1:]:
+        copy.start()
 
     def push_all(src, dst, sem):
         push(whole_group, sample, src, dst, send.at[sem], recv.at[sem], True)

time: 59.9 us -> 59.8 us (level)
  no operation moved by 1% of the time
where the time goes in v6:
time: 59.8 us; the launch traced here: 59.7 us
  Pallas kernels  58.9 us (98%)
  between operations  0.8 us (1%)
    pallas_call x1, Pallas kernels, body(): pl.pallas_call(kernel, out_shape=tuple((pltpu.VMEM(result.shape, result.d...  58 us

profile of v6, /device:TPU:1, one launch (start us, length us, event | category | flops | bytes accessed | tf_op | source)
XLA Modules:
  0.0 59.7 jit_solution(6875865773798182250)
XLA Ops:
  0.6 58.0 %evoformer_backward.1 = (bf16[512,256]{1,0:T(8,128)(2,1)S(1)}, f32[1024,128]{1,0:T(8,128)S(1)}, f32[64,256]{1,0:T(8,128)S(1)}, f32[128,128]{1,0:T(8,128)S(1)}) custom-call(bf16[512,256]{1,0:T(8,128)(2,1)} %bitcast.11, bf16[256,256]{1,0:T(8,128)(2,1)} %wq_in.1, bf16[256,256]{1,0:T(8,128)(2,1)} %wk_in.1, bf16[256,256]{1,0:T(8,128)(2,1)} %wv_in.1, ...), custom_call_target="tpu_custom_call" | custom-call | tf_op jit(solution)/shard_map/evoformer_backward/pallas_call | solution.py:520
  58.6 0.9 %settle.1 = (bf16[512,256]{1,0:T(8,128)(2,1)}, f32[1024,128]{1,0:T(8,128)}, f32[64,256]{1,0:T(8,128)}, f32[128,128]{1,0:T(8,128)}) custom-call(bf16[512,256]{1,0:T(8,128)(2,1)S(1)} %get-tuple-element.12.refs_0_, f32[1024,128]{1,0:T(8,128)S(1)} %get-tuple-element.13.refs_1_, f32[64,256]{1,0:T(8,128)S(1)} %get-tuple-element.14.refs_2_, ...), custom_call_target="tpu_custom_call" | custom-call | tf_op jit(solution)/shard_map/settle/pallas_call | solution.py:545
